TPU v7x, 32 devices: a whole 2x2x4 slice. The times are simulated.
32 devices in a mesh: cuts: 2 (over x), row: 16 (over z, y, core).
Axes of the slice: x: 2, y: 2, z: 4, core: 2. Of those that a mesh axis runs over, the one named last changes fastest.
Arguments:
- left_stem: bfloat16 [2, 8192, 4096], P(None, ('cuts', 'row')), parts along dimension 1, may hold values from -6 to 6
- right_stem: bfloat16 [2, 1024, 4096], P(None, ('cuts', 'row')), parts along dimension 1, may hold values from -6 to 6
- branches: bfloat16 [10, 2, 2, 512, 512], P(None, None, None, 'row'), may hold values from -0.1875 to 0.1875
- slice_bits: int32 [20], P('cuts'), parts along dimension 0, may hold values from 0 to 1
- perms: int32 [10, 8], P('cuts'), parts along dimension 0, may hold values from 0 to 7, each once within a row
Outputs:
- amplitude: float32 [2, 8192, 512], P(None, ('cuts', 'row')), parts along dimension 1
There are 2 independent parts, one for each index of `cuts`. A program takes and returns all parts, laid end to end along the dimension named above; an argument that names none is the same for every part. Nothing has to cross between parts.
Inputs may be any that keep to these rules, and one draw needn't show every extreme that they name: `perms`: each row holds every group number once.
All inputs are finite; a program needn't handle non-finite values.
Results may differ from a plain program's by a relative error of at most 0.012.
Values may be sent and summed in bfloat16 or wider, within the bound.
A program may use at most 64 MiB of HBM per device.

v0:
```python
import jax
import jax.numpy as jnp
from jax import lax
from jax.sharding import PartitionSpec as P


def column_mix(stem_in, matrix, strided):
    planes, rows, cols = stem_in.shape
    width = matrix.shape[-1]
    if strided:
        x_real = stem_in[0].reshape(rows, width, cols // width)
        x_imag = stem_in[1].reshape(rows, width, cols // width)

        def product(left_op, right_op):
            return jnp.einsum("mcg,cd->mdg", left_op, right_op, preferred_element_type=jnp.float32)

    else:
        x_real = stem_in[0].reshape(-1, width)
        x_imag = stem_in[1].reshape(-1, width)

        def product(left_op, right_op):
            return jnp.dot(left_op, right_op, preferred_element_type=jnp.float32)

    real_part = product(x_real, matrix[0]) - product(x_imag, matrix[1])
    imag_part = product(x_real, matrix[1]) + product(x_imag, matrix[0])
    return jnp.stack([real_part, imag_part]).reshape(planes, rows, cols).astype(jnp.bfloat16)


def row_mix(stem_in, matrix, strided):
    planes, rows, cols = stem_in.shape
    width = matrix.shape[-1]
    groups = rows // width
    if strided:
        y_real = stem_in[0].reshape(width, groups, cols)
        y_imag = stem_in[1].reshape(width, groups, cols)
        form = "rs,sgn->rgn"
    else:
        y_real = stem_in[0].reshape(groups, width, cols)
        y_imag = stem_in[1].reshape(groups, width, cols)
        form = "rs,hsn->hrn"
    real_part = jnp.einsum(
        form, matrix[0], y_real, preferred_element_type=jnp.float32
    ) - jnp.einsum(form, matrix[1], y_imag, preferred_element_type=jnp.float32)
    imag_part = jnp.einsum(
        form, matrix[0], y_imag, preferred_element_type=jnp.float32
    ) + jnp.einsum(form, matrix[1], y_real, preferred_element_type=jnp.float32)
    return jnp.stack([real_part, imag_part]).reshape(planes, rows, cols).astype(jnp.bfloat16)


def permute(stem_in, block_order):
    planes, rows, cols = stem_in.shape
    blocks = block_order.shape[0]
    blocked = stem_in.reshape(planes, rows, blocks, cols // blocks)
    return jnp.take(blocked, block_order, axis=2).reshape(planes, rows, cols)


def sweep_apply(stem_rows, col_matrix, row_matrix, block_order, strided):
    mixed = column_mix(stem_rows, col_matrix, strided)
    spread = lax.all_to_all(mixed, "row", split_axis=2, concat_axis=1, tiled=True)
    turned = row_mix(spread, row_matrix, strided)
    rows_again = lax.all_to_all(turned, "row", split_axis=1, concat_axis=2, tiled=True)
    return permute(rows_again, block_order)


def join_block(left, scale, piece):
    contract = (((1,), (1,)), ((), ()))
    real_part = lax.dot_general(
        left[0], piece[0], contract, preferred_element_type=jnp.float32
    ) - lax.dot_general(left[1], piece[1], contract, preferred_element_type=jnp.float32)
    imag_part = lax.dot_general(
        left[0], piece[1], contract, preferred_element_type=jnp.float32
    ) + lax.dot_general(left[1], piece[0], contract, preferred_element_type=jnp.float32)
    return jnp.stack([real_part, imag_part]) * scale


def shards(left_stem, right_stem, branches, slice_bits, perms):

    def fetch_branch(index):
        chosen = lax.dynamic_index_in_dim(branches[index], slice_bits[index], 0, keepdims=False)
        return lax.all_gather(chosen, "row", axis=1, tiled=True)

    left_sweeps = 3
    right_sweeps = 2
    left = left_stem
    for sweep in range(left_sweeps):
        left = sweep_apply(
            left, fetch_branch(2 * sweep), fetch_branch(2 * sweep + 1), perms[sweep], sweep % 2 == 1
        )
    scale = (2.0 * left_stem.shape[2]) ** (-0.5)
    last = left_sweeps + right_sweeps - 1
    right = right_stem
    sweep = 3
    right = sweep_apply(
        right, fetch_branch(2 * sweep), fetch_branch(2 * sweep + 1), perms[sweep], sweep % 2 == 1
    )
    right = sweep_apply(
        right, fetch_branch(2 * last), fetch_branch(2 * last + 1), perms[last], last % 2 == 1
    )
    return join_block(left, scale, lax.all_gather(right, "row", axis=1, tiled=True))


def solution(mesh):
    in_specs = (
        P(None, ("cuts", "row"), None),
        P(None, ("cuts", "row"), None),
        P(None, None, None, "row", None),
        P("cuts"),
        P("cuts", None),
    )
    out_specs = P(None, ("cuts", "row"), None)
    return jax.shard_map(shards, mesh=mesh, in_specs=in_specs, out_specs=out_specs, check_vma=False)
```

profile of v0, /device:TPU:13, one launch (start us, length us, event | category | flops | bytes accessed | tf_op | source)
XLA Modules:
  0.0 1158.0 jit_solution(7568064394036765262)
XLA Ops:
  12.0 3.9 fusion.80
  21.2 29.2 %all-gather.28.cloned.1.call-done = bf16[1,1,2,512,512]{4,3,2,1,0:T(8,128)(2,1)} async-done(((bf16[1,1,2,32,512]{4,3,2,1,0:T(8,128)(2,1)}), bf16[1,1,2,512,512]{4,3,2,1,0:T(8,128)(2,1)}) %all-gather.28.cloned.1.call-update) | async-done | bytes 1048592 | tf_op jit(solution)/shard_map/all_gather | solution.py:80
  50.5 3.1 fusion.53
  56.3 4.0 copy.383
  60.2 4.2 stack.106
  75.2 4.6 pad_maximum_fusion
  79.8 11.1 copy.384
  91.0 6.1 all-to-all-start
  105.2 69.7 %all-gather.38.cloned.1.call-done = bf16[1,1,2,512,512]{4,3,2,1,0:T(8,128)(2,1)} async-done(((bf16[1,1,2,32,512]{4,3,2,1,0:T(8,128)(2,1)}), bf16[1,1,2,512,512]{4,3,2,1,0:T(8,128)(2,1)}) %all-gather.38.cloned.1.call-update) | async-done | bytes 1048592 | tf_op jit(solution)/shard_map/all_gather | solution.py:80
  180.2 17.8 %copy.530 = bf16[2,32,4096]{1,0,2:T(2,128)(2,1)S(1)} copy(bf16[2,32,4096]{1,2,0:T(8,128)(2,1)S(1)} %pad_maximum_fusion.6) | data formatting | bytes 1048576 | tf_op jit(solution)/shard_map/stack | solution.py:26
  200.7 8.3 all-to-all-start.6
  217.0 3.9 copy.386
  228.1 3.9 copy.393
  232.0 2.9 fusion.55
  237.7 4.1 copy.390
  243.7 27.2 %copy.394 = bf16[2,4096,256]{2,0,1:T(2,128)(2,1)} copy(bf16[2,4096,256]{2,1,0:T(8,128)(2,1)S(1)} %pad_maximum_fusion.1) | data formatting | bytes 8388608 | tf_op jit(solution)/shard_map/stack | solution.py:47
  270.9 4.8 all-to-all-start.1
  281.8 71.8 %all-gather.26.cloned.1.call-done = bf16[1,1,2,512,512]{4,2,1,0,3:T(2,128)(2,1)} async-done(((bf16[1,1,2,32,512]{4,2,1,0,3:T(2,128)(2,1)}), bf16[1,1,2,512,512]{4,2,1,0,3:T(2,128)(2,1)}) %all-gather.26.cloned.1.call-update) | async-done | bytes 1048592 | tf_op jit(solution)/shard_map/all_gather | solution.py:80
  353.5 3.3 fusion.82
  359.5 5.1 reshape.317
  368.0 29.2 %all-gather.36.cloned.1.call-done = bf16[1,1,2,512,512]{4,3,2,1,0:T(8,128)(2,1)} async-done(((bf16[1,1,2,32,512]{4,3,2,1,0:T(8,128)(2,1)}), bf16[1,1,2,512,512]{4,3,2,1,0:T(8,128)(2,1)}) %all-gather.36.cloned.1.call-update) | async-done | bytes 1048592 | tf_op jit(solution)/shard_map/all_gather | solution.py:80
  402.0 5.6 all-to-all-start.7
  407.6 4.7 copy.395
  412.4 6.2 copy.396
  418.6 6.2 copy.397
  424.8 5.0 gather_fusion
  440.6 3.9 copy.401
  444.5 3.0 copy.402
  447.5 3.0 fusion.49
  457.3 27.6 %copy.407 = bf16[2,256,4096]{1,0,2:T(2,128)(2,1)} copy(bf16[2,256,4096]{1,2,0:T(8,128)(2,1)S(1)} %pad_maximum_fusion.2) | data formatting | bytes 8388608 | tf_op jit(solution)/shard_map/stack | solution.py:26
  484.9 6.2 all-to-all-start.2
  498.7 70.2 %all-gather.40.cloned.1.call-done = bf16[1,1,2,512,512]{4,3,2,1,0:T(8,128)(2,1)} async-done(((bf16[1,1,2,32,512]{4,3,2,1,0:T(8,128)(2,1)}), bf16[1,1,2,512,512]{4,3,2,1,0:T(8,128)(2,1)}) %all-gather.40.cloned.1.call-update) | async-done | bytes 1048592 | tf_op jit(solution)/shard_map/all_gather | solution.py:80
  578.1 14.0 %all-to-all-done.2 = bf16[2,256,4096]{1,0,2:T(2,128)(2,1)} async-done(((bf16[2,256,4096]{1,0,2:T(2,128)(2,1)}), bf16[2,256,4096]{1,0,2:T(2,128)(2,1)}, u32[]{:S(2)}, u32[]{:S(2)}) %all-to-all-start.2) | async-done | bytes 4194336 | tf_op jit(solution)/shard_map/all_to_all | solution.py:59
  592.1 4.6 all-to-all-start.8
  604.6 4.0 copy.409
  608.6 6.8 all-gather.24.cloned.1.call-done
  624.5 27.2 %copy.417 = bf16[2,4096,256]{2,0,1:T(2,128)(2,1)} copy(bf16[2,4096,256]{2,1,0:T(8,128)(2,1)S(1)} %pad_maximum_fusion.3) | data formatting | bytes 8388608 | tf_op jit(solution)/shard_map/stack | solution.py:47
  651.7 4.7 all-to-all-start.3
  664.1 70.1 %all-gather.42.cloned.1.call-done = bf16[1,1,2,512,512]{4,3,2,1,0:T(8,128)(2,1)} async-done(((bf16[1,1,2,32,512]{4,3,2,1,0:T(8,128)(2,1)}), bf16[1,1,2,512,512]{4,3,2,1,0:T(8,128)(2,1)}) %all-gather.42.cloned.1.call-update) | async-done | bytes 1048592 | tf_op jit(solution)/shard_map/all_gather | solution.py:80
  739.0 18.5 %all-to-all-done.3 = bf16[2,4096,256]{2,0,1:T(2,128)(2,1)} async-done(((bf16[2,4096,256]{2,0,1:T(2,128)(2,1)}), bf16[2,4096,256]{2,0,1:T(2,128)(2,1)}, u32[]{:S(2)}, u32[]{:S(2)}) %all-to-all-start.3) | async-done | bytes 4194336 | tf_op jit(solution)/shard_map/all_to_all | solution.py:61
  757.5 5.0 all-to-all-start.9
  762.5 4.7 copy.418
  767.2 6.3 copy.419
  773.5 6.3 copy.420
  779.7 5.0 gather_fusion.1
  793.4 3.0 add_convert_fusion.1
  798.2 4.2 stack.118
  802.4 10.1 copy.424
  814.8 10.1 copy.423
  824.8 10.9 pad_maximum_fusion.4
  835.7 6.1 all-to-all-start.4
  847.4 106.8 %all-to-all-done.4 = bf16[2,256,4096]{1,0,2:T(2,128)(2,1)} async-done(((bf16[2,256,4096]{1,0,2:T(2,128)(2,1)}), bf16[2,256,4096]{1,0,2:T(2,128)(2,1)}, u32[]{:S(2)}, u32[]{:S(2)}) %all-to-all-start.4) | async-done | bytes 4194336 | tf_op jit(solution)/shard_map/all_to_all | solution.py:59
  962.0 4.0 copy.426
  971.2 3.9 copy.433
  975.1 3.0 fusion.57
  980.8 4.1 copy.430
  986.9 25.5 %copy.434 = bf16[2,4096,256]{2,0,1:T(2,128)(2,1)S(1)} copy(bf16[2,4096,256]{2,1,0:T(8,128)(2,1)S(1)} %pad_maximum_fusion.5) | data formatting | bytes 8388608 | tf_op jit(solution)/shard_map/stack | solution.py:47
  1012.4 96.2 %all_to_all.150 = bf16[2,4096,256]{2,0,1:T(2,128)(2,1)S(1)} all-to-all(bf16[2,4096,256]{2,0,1:T(2,128)(2,1)S(1)} %copy.434), channel_id=1, replica_groups=mesh['cuts'=2,'row'=16] {'row'}, dimensions={1} | all-to-all | bytes 8388608 | tf_op jit(solution)/shard_map/all_to_all | solution.py:61
  1111.1 6.2 copy.436
  1117.3 6.3 copy.437
  1123.6 5.1 gather_fusion.2
  1133.0 3.9 copy.465
  1139.3 4.3 fusion
  1143.6 3.6 fusion.1
  (233 shorter events, 170.2 us)
Async XLA Ops:
  6.5 2.3 copy-start.24
  6.5 43.9 %all-gather.28.cloned.1.call-start = ((), (), s32[]{:S(2)}) async-start(), calls=%async_computation.13 | async-start | bytes 1114112 | tf_op jit(solution)/shard_map/all_gather | solution.py:80
  50.4 3.2 copy-start.7
  91.0 8.2 copy-start.23
  91.0 11.1 copy-start.22
  91.0 11.8 %copy-start.17 = (bf16[2,32,4096]{2,1,0:T(8,128)(2,1)S(1)}, bf16[2,32,4096]{2,1,0:T(8,128)(2,1)}, u32[]{:S(2)}) copy-start(bf16[2,32,4096]{2,1,0:T(8,128)(2,1)} %param.10) | copy-start | bytes 1572868
  91.0 109.7 %all-to-all-start = ((bf16[2,256,4096]{1,0,2:T(2,128)(2,1)}), bf16[2,256,4096]{1,0,2:T(2,128)(2,1)}, u32[]{:S(2)}, u32[]{:S(2)}) async-start(bf16[2,256,4096]{1,0,2:T(2,128)(2,1)} %copy.384), calls=%async_computation | async-start | bytes 8388608 | tf_op jit(solution)/shard_map/all_to_all | solution.py:59
  97.1 77.8 %all-gather.38.cloned.1.call-start = ((), (), s32[]{:S(2)}) async-start(), calls=%async_computation.18 | async-start | bytes 1114112 | tf_op jit(solution)/shard_map/all_gather | solution.py:80
  99.9 122.9 %all-gather.30.cloned.1.call-start = ((), (), s32[]{:S(2)}) async-start(), calls=%async_computation.14 | async-start | bytes 1114112 | tf_op jit(solution)/shard_map/all_gather | solution.py:80
  174.9 1.4 copy-start.32
  177.4 1.2 copy-start.33
  200.7 70.2 %all-to-all-start.6 = ((bf16[16,2,8192]{2,1,0:T(2,128)(2,1)}), bf16[16,2,8192]{2,1,0:T(2,128)(2,1)}, u32[]{:S(2)}, u32[]{:S(2)}) async-start(bf16[16,2,8192]{2,1,0:T(2,128)(2,1)} %reshape.316), calls=%async_computation.6 | async-start | bytes 1048576 | tf_op jit(solution)/shard_map/all_to_all | solution.py:59
  222.8 2.5 copy-start.2
  222.8 2.5 copy-start.12
  237.7 4.1 copy-start.5
  270.9 6.7 copy-start.21
  270.9 9.6 copy-start.20
  270.9 10.3 copy-start.31
  270.9 131.1 %all-to-all-start.1 = ((bf16[2,4096,256]{2,0,1:T(2,128)(2,1)}), bf16[2,4096,256]{2,0,1:T(2,128)(2,1)}, u32[]{:S(2)}, u32[]{:S(2)}) async-start(bf16[2,4096,256]{2,0,1:T(2,128)(2,1)} %copy.394), calls=%async_computation.1 | async-start | bytes 8388608 | tf_op jit(solution)/shard_map/all_to_all | solution.py:61
  275.8 77.8 %all-gather.26.cloned.1.call-start = ((), (), s32[]{:S(2)}) async-start(), calls=%async_computation.12 | async-start | bytes 1114112 | tf_op jit(solution)/shard_map/all_gather | solution.py:80
  278.4 118.8 %all-gather.36.cloned.1.call-start = ((), (), s32[]{:S(2)}) async-start(), calls=%async_computation.17 | async-start | bytes 1114112 | tf_op jit(solution)/shard_map/all_gather | solution.py:80
  397.2 2.8 copy-start.10
  402.0 82.9 %all-to-all-start.7 = ((bf16[2,512,256]{2,0,1:T(2,128)(2,1)}), bf16[2,512,256]{2,0,1:T(2,128)(2,1)}, u32[]{:S(2)}, u32[]{:S(2)}) async-start(bf16[2,512,256]{2,0,1:T(2,128)(2,1)} %copy.451), calls=%async_computation.7 | async-start | bytes 1048576 | tf_op jit(solution)/shard_map/all_to_all | solution.py:61
  424.8 5.0 copy-start.26
  447.5 3.0 copy-start.4
  484.9 8.3 copy-start.19
  484.9 11.3 copy-start.29
  484.9 11.3 copy-start.30
  484.9 107.2 %all-to-all-start.2 = ((bf16[2,256,4096]{1,0,2:T(2,128)(2,1)}), bf16[2,256,4096]{1,0,2:T(2,128)(2,1)}, u32[]{:S(2)}, u32[]{:S(2)}) async-start(bf16[2,256,4096]{1,0,2:T(2,128)(2,1)} %copy.407), calls=%async_computation.2 | async-start | bytes 8388608 | tf_op jit(solution)/shard_map/all_to_all | solution.py:59
  491.1 77.8 %all-gather.40.cloned.1.call-start = ((), (), s32[]{:S(2)}) async-start(), calls=%async_computation.19 | async-start | bytes 1114112 | tf_op jit(solution)/shard_map/all_gather | solution.py:80
  493.9 121.5 %all-gather.24.cloned.1.call-start = ((), (), s32[]{:S(2)}) async-start(), calls=%async_computation.11 | async-start | bytes 1114112 | tf_op jit(solution)/shard_map/all_gather | solution.py:80
  568.9 2.9 copy-start.9
  592.1 59.6 %all-to-all-start.8 = ((bf16[16,2,8192]{2,1,0:T(2,128)(2,1)}), bf16[16,2,8192]{2,1,0:T(2,128)(2,1)S(1)}, u32[]{:S(2)}, u32[]{:S(2)}) async-start(bf16[16,2,8192]{2,1,0:T(2,128)(2,1)} %reshape.318), calls=%async_computation.8 | async-start | bytes 1048576 | tf_op jit(solution)/shard_map/all_to_all | solution.py:59
  615.4 2.5 copy-start
  615.4 2.5 copy-start.14
  651.7 9.9 copy-start.27
  651.7 9.9 copy-start.28
  651.7 105.8 %all-to-all-start.3 = ((bf16[2,4096,256]{2,0,1:T(2,128)(2,1)}), bf16[2,4096,256]{2,0,1:T(2,128)(2,1)}, u32[]{:S(2)}, u32[]{:S(2)}) async-start(bf16[2,4096,256]{2,0,1:T(2,128)(2,1)} %copy.417), calls=%async_computation.3 | async-start | bytes 8388608 | tf_op jit(solution)/shard_map/all_to_all | solution.py:61
  656.4 77.8 %all-gather.42.cloned.1.call-start = ((), (), s32[]{:S(2)}) async-start(), calls=%async_computation.20 | async-start | bytes 1114112 | tf_op jit(solution)/shard_map/all_gather | solution.py:80
  658.8 130.3 %all-gather.32.cloned.1.call-start = ((), (), s32[]{:S(2)}) async-start(), calls=%async_computation.15 | async-start | bytes 1114112 | tf_op jit(solution)/shard_map/all_gather | solution.py:80
  734.2 2.9 copy-start.11
  757.5 78.2 %all-to-all-start.9 = ((bf16[2,512,256]{2,0,1:T(2,128)(2,1)}), bf16[2,512,256]{2,0,1:T(2,128)(2,1)S(1)}, u32[]{:S(2)}, u32[]{:S(2)}) async-start(bf16[2,512,256]{2,0,1:T(2,128)(2,1)} %copy.460), calls=%async_computation.9 | async-start | bytes 1048576 | tf_op jit(solution)/shard_map/all_to_all | solution.py:61
  789.1 2.7 copy-start.8
  791.8 1.6 copy-start.1
  835.7 8.2 copy-start.18
  835.7 118.5 %all-to-all-start.4 = ((bf16[2,256,4096]{1,0,2:T(2,128)(2,1)}), bf16[2,256,4096]{1,0,2:T(2,128)(2,1)}, u32[]{:S(2)}, u32[]{:S(2)}) async-start(bf16[2,256,4096]{1,0,2:T(2,128)(2,1)} %pad_maximum_fusion.4), calls=%async_computation.4 | async-start | bytes 8388608 | tf_op jit(solution)/shard_map/all_to_all | solution.py:59
  841.8 124.1 %all-gather.34.cloned.1.call-start = ((), (), s32[]{:S(2)}) async-start(), calls=%async_computation.16 | async-start | bytes 1114112 | tf_op jit(solution)/shard_map/all_gather | solution.py:80
  844.6 294.7 %all-gather.22.cloned.1.call-start = ((), (), s32[]{:S(2)}) async-start(), calls=%async_computation.10 | async-start | bytes 8912896 | tf_op jit(solution)/shard_map/all_gather | solution.py:99
  966.0 2.5 copy-start.3
  966.0 2.5 copy-start.13
  980.8 4.1 copy-start.6
  1123.6 5.1 copy-start.25
  1139.3 4.3 copy-start.16
  1139.3 7.9 slice-start
  1143.6 3.7 slice-start.1
  1147.3 1.6 copy-start.15
Sparse Core Ops, SparseCore 0:
  12.1 38.2 all-gather.27
  100.1 74.7 all-gather.37
  177.1 45.6 all-gather.29
  278.5 74.9 all-gather.25
  355.6 41.5 all-gather.35
  494.0 74.8 all-gather.39
  571.1 44.2 all-gather.23
  659.5 74.7 all-gather.41
  736.4 44.2 all-gather.31
  844.7 74.8 all-gather.33
  921.8 80.9 all-gather.21
where the time goes:
time: 1170 us; the launch traced here: 1160 us
  waiting for transfers between devices  488 us (42%)
  local copies, waits for them, and re-layouts  378 us (32%)
  blocking collectives  96.2 us (8%)
  matrix products  78.4 us (7%)
  starting transfers between devices  52.9 us (5%)
  between operations  33.3 us (3%)
  other arithmetic  30.7 us (3%)
    all_gather x10, waiting for transfers between devices, fetch_branch(): return lax.all_gather(chosen, 'row', axis=1, tiled=True)  349 us
    all_to_all x5, waiting for transfers between devices, sweep_apply(): lax.all_to_all(mixed, 'row', split_axis=2, concat_axis=1, tiled=True)  121 us
    all_to_all x1, blocking collectives, sweep_apply(): lax.all_to_all(turned, 'row', split_axis=1, concat_axis=2, tiled=True)  96.2 us
    another operation x13, local copies, waits for them, and re-layouts, column_mix(): jnp.stack([real_part, imag_part]).reshape(planes, rows, cols)  95.3 us
    another operation x3, local copies, waits for them, and re-layouts, row_mix(): jnp.stack([real_part, imag_part]).reshape(planes, rows, cols)  79.9 us
    all_to_all x9, local copies, waits for them, and re-layouts, sweep_apply(): lax.all_to_all(turned, 'row', split_axis=1, concat_axis=2, tiled=True)  32.4 us
    all_to_all x5, starting transfers between devices, sweep_apply(): lax.all_to_all(mixed, 'row', split_axis=2, concat_axis=1, tiled=True)  31.4 us
    dot_general x12, matrix products, product(): return jnp.dot(left_op, right_op, preferred_element_type=jnp.float32)  23.7 us
  transfers between devices with their start and end apart: 20, of which 11 were waited for; matrix products, arithmetic and copies ran while one was open for 37% of the time, Pallas kernels for 0%

commit v1 on v0

v1 whole, which is shorter than its diff:
```python
import jax
import jax.numpy as jnp
from jax import lax
from jax.sharding import PartitionSpec as P


def packed(matrix, transposed):
    real, imag = matrix[0], matrix[1]
    if transposed:
        real, imag = real.T, imag.T
    top = jnp.concatenate([real, imag], axis=1)
    bottom = jnp.concatenate([-imag, real], axis=1)
    return jnp.concatenate([top, bottom], axis=0)


def mix(rows_in, matrix, strided, transposed):
    planes, rows, cols = rows_in.shape
    width = matrix.shape[-1]
    groups = cols // width
    if strided:
        grouped = rows_in.reshape(planes, rows, width, groups)
        flat = grouped.transpose(1, 3, 0, 2).reshape(rows * groups, planes * width)
    else:
        grouped = rows_in.reshape(planes, rows, groups, width)
        flat = grouped.transpose(1, 2, 0, 3).reshape(rows * groups, planes * width)
    mixed = jnp.dot(flat, packed(matrix, transposed), preferred_element_type=jnp.float32)
    mixed = mixed.astype(jnp.bfloat16).reshape(rows, groups, planes, width)
    if strided:
        return mixed.transpose(2, 0, 3, 1).reshape(planes, rows, cols)
    return mixed.transpose(2, 0, 1, 3).reshape(planes, rows, cols)


def permute(stem_in, block_order):
    planes, rows, cols = stem_in.shape
    blocks = block_order.shape[0]
    blocked = stem_in.reshape(planes, rows, blocks, cols // blocks)
    return jnp.take(blocked, block_order, axis=2).reshape(planes, rows, cols)


def contract(left, right, dims):
    def dot(a, b):
        return lax.dot_general(a, b, (dims, ((), ())), preferred_element_type=jnp.float32)

    real_part = dot(left[0], right[0]) - dot(left[1], right[1])
    imag_part = dot(left[0], right[1]) + dot(left[1], right[0])
    return jnp.stack([real_part, imag_part])


def shards(left_stem, right_stem, branches, slice_bits, perms):
    left_sweeps = 3
    sweeps = perms.shape[0]

    def own(index):
        return lax.dynamic_index_in_dim(branches[index], slice_bits[index], 0, keepdims=False)

    def fetch(indices):
        stacked = jnp.stack([own(index) for index in indices])
        return lax.all_gather(stacked, "row", axis=2, tiled=True)

    col_mats = fetch([2 * s for s in range(sweeps)])
    row_mats = fetch([2 * s + 1 for s in range(sweeps)])

    stem = right_stem
    for s in range(left_sweeps, sweeps):
        stem = permute(mix(stem, col_mats[s], s % 2 == 1, False), perms[s])
    for s in reversed(range(left_sweeps)):
        stem = permute(stem, jnp.argsort(perms[s]))
        stem = mix(stem, col_mats[s], s % 2 == 1, True)
    gathered = lax.all_gather(stem, "row", axis=1, tiled=True)

    joined = contract(gathered, left_stem, ((1,), (1,))).astype(jnp.bfloat16)
    spread = lax.all_to_all(joined, "row", split_axis=1, concat_axis=2, tiled=True)
    for s in range(left_sweeps):
        spread = mix(spread, row_mats[s], s % 2 == 1, True)
    turned = lax.all_to_all(spread, "row", split_axis=2, concat_axis=1, tiled=True)

    right_rows = row_mats[left_sweeps]
    for s in range(left_sweeps + 1, sweeps):
        right_rows = contract(row_mats[s], right_rows, ((1,), (0,))).astype(jnp.bfloat16)
    scale = (2.0 * left_stem.shape[2]) ** (-0.5)
    return contract(turned, right_rows, ((0,), (1,))) * scale


def solution(mesh):
    in_specs = (
        P(None, ("cuts", "row"), None),
        P(None, ("cuts", "row"), None),
        P(None, None, None, "row", None),
        P("cuts"),
        P("cuts", None),
    )
    out_specs = P(None, ("cuts", "row"), None)
    return jax.shard_map(shards, mesh=mesh, in_specs=in_specs, out_specs=out_specs, check_vma=False)
```

time: 1170 us -> 317 us (0.27)
  waiting for transfers between devices: 488 us -> 163 us
  local copies, waits for them, and re-layouts: 378 us -> 60.7 us
  blocking collectives: 96.2 us -> 0 us
  matrix products: 78.4 us -> 32.4 us
  starting transfers between devices: 52.9 us -> 10.7 us
  other arithmetic: 30.7 us -> 14.4 us
    all_gather x11 -> x3, waiting for transfers between devices: 349 us -> 156 us  [the longest x2 93.4 us: fetch(): return lax.all_gather(stacked, 'row', axis=2, tiled=True)]
    another operation x24 -> x5, local copies, waits for them, and re-layouts: 190 us -> 3.13 us  [the longest x2 1.77 us: permute(): blocked = stem_in.reshape(planes, rows, blocks, cols // blocks)]
    all_to_all x9 -> x2, waiting for transfers between devices: 139 us -> 7.17 us  [the longest x1 7.16 us: shards(): lax.all_to_all(spread, 'row', split_axis=2, concat_axis=1, tiled=True)]
    all_to_all x1 -> x0, blocking collectives: 96.2 us -> none  [sweep_apply(): lax.all_to_all(turned, 'row', split_axis=1, concat_axis=2, tiled=True)]
    slice x30 -> x5, local copies, waits for them, and re-layouts: 58.9 us -> 5.14 us  [the longest x1 2.2 us: own(): branches[index]]
    dot_general x44 -> x20, matrix products: 78.4 us -> 32.4 us  [the longest x12 17.8 us: dot(): lax.dot_general(a, b, (dims, ((), ())), preferred_element_type=jnp.float32)]
    all_to_all x14 -> x2, local copies, waits for them, and re-layouts: 44 us -> 2.45 us  [the longest x1 2.16 us: shards(): lax.all_to_all(spread, 'row', split_axis=2, concat_axis=1, tiled=True)]
    all_to_all x9 -> x2, starting transfers between devices: 51.7 us -> 10.7 us  [the longest x1 5.33 us: shards(): lax.all_to_all(joined, 'row', split_axis=1, concat_axis=2, tiled=True)]
  transfers between devices with their start and end apart: 20 -> 5, of which waited for: 11 -> 4; matrix products, arithmetic and copies ran while one was open for 37% -> 10% of each run, Pallas kernels for 0% -> 0%
where the time goes in v1:
time: 317 us; the launch traced here: 314 us
  waiting for transfers between devices  163 us (51%)
  local copies, waits for them, and re-layouts  60.7 us (19%)
  between operations  32.9 us (10%)
  matrix products  32.4 us (10%)
  other arithmetic  14.4 us (5%)
  starting transfers between devices  10.7 us (3%)
    all_gather x2, waiting for transfers between devices, fetch(): return lax.all_gather(stacked, 'row', axis=2, tiled=True)  93.4 us
    all_gather x1, waiting for transfers between devices, shards(): gathered = lax.all_gather(stem, 'row', axis=1, tiled=True)  62.6 us
    unnamed x55, local copies, waits for them, and re-layouts  20.8 us
    dot_general x12, matrix products, dot(): lax.dot_general(a, b, (dims, ((), ())), preferred_element_type=jnp.float32)  17.8 us
    dot_general x8, matrix products, mix(): jnp.dot(flat, packed(matrix, transposed), preferred_element_type=jnp.floa...  14.6 us
    reshape x6, local copies, waits for them, and re-layouts, mix(): mixed = mixed.astype(jnp.bfloat16).reshape(rows, groups, planes, width)  8.41 us
    transpose x2, local copies, waits for them, and re-layouts, packed(): real, imag = (real.T, imag.T)  7.45 us
    neg x3, other arithmetic, packed(): bottom = jnp.concatenate([-imag, real], axis=1)  7.2 us
  transfers between devices with their start and end apart: 5, of which 4 were waited for; matrix products, arithmetic and copies ran while one was open for 10% of the time, Pallas kernels for 0%

profile of v1, /device:TPU:13, one launch (start us, length us, event | category | flops | bytes accessed | tf_op | source)
XLA Modules:
  0.0 314.2 jit_solution(11146656162412084216)
XLA Ops:
  6.5 1.7 fusion.145
  14.6 2.2 fusion.143
  20.0 0.7 copy-done.7
  20.8 1.9 copy.52
  22.7 1.9 copy.81
  24.7 1.0 sort.45
  25.7 1.0 sort.47
  26.8 1.0 sort.46
  27.8 0.6 compare_and_fusion.3
  28.4 0.6 pad_clamp_fusion.4
  29.6 48.0 %all-gather.4.cloned.1.call-done = bf16[5,2,512,512]{3,2,1,0:T(8,128)(2,1)} async-done(((bf16[5,2,32,512]{3,2,1,0:T(8,128)(2,1)}), bf16[5,2,512,512]{3,2,1,0:T(8,128)(2,1)}) %all-gather.4.cloned.1.call-update) | async-done | bytes 5242896 | tf_op jit(solution)/shard_map/all_gather | solution.py:58
  77.6 4.4 %slice_bitcast_fusion.28 = (bf16[512,512]{0,1:T(8,128)(2,1)S(1)}, bf16[512,512]{0,1:T(8,128)(2,1)}, bf16[512,512]{0,1:T(8,128)(2,1)}, bf16[512,512]{0,1:T(8,128)...) fusion(bf16[5,2,512,512]{3,2,1,0:T(8,128)(2,1)} %all-gather.4.c, ...), kind=kLoop, calls=%fused_computation.117 | loop fusion | bytes 10485760 | tf_op jit(solution)/shard_map/transpose | solution.py:10
  81.9 2.1 fusion.136
  84.0 0.8 fusion.102
  85.4 1.8 copy.55
  87.2 0.8 copy.56
  88.0 0.8 gather_fusion
  88.9 0.8 select_bitcast_fusion.4
  89.6 0.5 copy.106
  90.3 0.7 fusion.94
  91.3 0.6 gather_fusion.1
  92.1 0.6 gather_fusion.2
  93.4 2.5 fusion.139
  96.0 0.7 fusion.91
  97.0 0.6 gather_fusion.3
  97.7 1.0 copy.62
  98.8 1.9 copy.84
  100.7 3.1 fusion.88
  103.8 2.7 copy.64
  106.6 1.0 copy.65
  107.6 0.6 gather_fusion.4
  108.9 0.7 fusion.85
  110.1 1.1 copy.79
  120.9 0.7 copy-done.8
  121.7 62.6 %all-gather.6.cloned.1.call-done = bf16[2,512,4096]{2,1,0:T(8,128)(2,1)} async-done(((bf16[2,32,4096]{2,1,0:T(8,128)(2,1)}), bf16[2,512,4096]{2,1,0:T(8,128)(2,1)}) %all-gather.6.cloned.1.call-update) | async-done | bytes 8388624 | tf_op jit(solution)/shard_map/all_gather | solution.py:69
  184.2 4.3 %fusion = f32[512,256]{1,0:T(8,128)S(1)} fusion(bf16[2,512,4096]{2,1,0:T(8,128)(2,1)} %all-gather.6.cloned.1.call-done, bf16[2,256,4096]{2,1,0:T(8,128)(2,1)} %param.7), kind=kOutput, calls=%fused_computation.7 | convolution fusion | flops 1073741824 | bytes 6815744 | tf_op jit(solution)/shard_map/dot_general | solution.py:42
  188.5 1.0 copy-done.16
  189.5 3.0 fusion.1
  192.5 1.3 fusion.122
  193.8 1.3 fusion.119
  195.2 1.3 copy.68
  196.5 5.3 %all-to-all-start = ((bf16[2,512,256]{2,0,1:T(2,128)(2,1)}), bf16[2,512,256]{2,0,1:T(2,128)(2,1)S(1)}, u32[]{:S(2)}, u32[]{:S(2)}) async-start(bf16[2,512,256]{2,0,1:T(2,128)(2,1)} %copy.68), calls=%async_computation | async-start | bytes 1048576 | tf_op jit(solution)/shard_map/all_to_all | solution.py:72
  201.8 45.4 %all-gather.8.cloned.1.call-done = bf16[5,2,512,512]{3,2,1,0:T(8,128)(2,1)} async-done(((bf16[5,2,32,512]{3,2,1,0:T(8,128)(2,1)}), bf16[5,2,512,512]{3,2,1,0:T(8,128)(2,1)}) %all-gather.8.cloned.1.call-update) | async-done | bytes 5242896 | tf_op jit(solution)/shard_map/all_gather | solution.py:58
  247.2 2.6 fusion.142
  249.8 3.1 slice_bitcast_fusion.22
  254.0 2.6 fusion.82
  256.6 2.0 copy.71
  258.6 2.6 copy.87
  261.2 3.2 %fusion.79 = bf16[256,1024]{1,0:T(8,128)(2,1)} fusion(bf16[256,1024]{1,0:T(8,128)(2,1)} %bitcast.326, bf16[512,512]{0,1:T(8,128)(2,1)} %get-tuple-element.19, bf16[512,512]{0,1:T(8,128)(2,1)} %get-tuple-element.23, bf16[512,512]{0,1:T(8,128)(2,1)} %get-tuple-element.18), kind=kOutput, calls=%fused_computation.86 | convolution fusion | flops 545521664 | bytes 2621440 | tf_op jit(solution)/shard_map/dot_general | solution.py:26
  264.4 2.7 copy.73
  267.1 1.8 copy.88
  268.9 2.7 fusion.76
  271.7 3.3 %copy.75 = bf16[2,32,8,512]{1,0,3,2:T(2,128)(2,1)S(1)} copy(bf16[2,32,8,512]{3,2,0,1:T(8,128)(2,1)} %bitcast.328) | data formatting | bytes 1048576 | tf_op jit(solution)/shard_map/transpose | solution.py:30
  274.9 2.7 reshape.198
  277.6 5.3 %all-to-all-start.1 = ((bf16[16,2,8192]{2,1,0:T(2,128)(2,1)}), bf16[16,2,8192]{2,1,0:T(2,128)(2,1)}, u32[]{:S(2)}, u32[]{:S(2)}) async-start(bf16[16,2,8192]{2,1,0:T(2,128)(2,1)} %reshape.198), calls=%async_computation.1 | async-start | bytes 1048576 | tf_op jit(solution)/shard_map/all_to_all | solution.py:75
  282.9 1.6 fusion.125
  284.5 1.6 fusion.126
  286.2 1.6 fusion.101
  287.8 1.6 fusion.100
  289.5 7.2 %all-to-all-done.1 = bf16[16,2,8192]{2,1,0:T(2,128)(2,1)} async-done(((bf16[16,2,8192]{2,1,0:T(2,128)(2,1)}), bf16[16,2,8192]{2,1,0:T(2,128)(2,1)}, u32[]{:S(2)}, u32[]{:S(2)}) %all-to-all-start.1) | async-done | bytes 524320 | tf_op jit(solution)/shard_map/all_to_all | solution.py:75
  296.6 5.1 %reshape.199 = bf16[4096,2,32]{2,1,0:T(2,128)(2,1)S(1)} reshape(bf16[16,2,8192]{2,1,0:T(2,128)(2,1)} %all-to-all-done.1) | data formatting | bytes 1048576
  301.7 2.2 copy.80
  303.9 1.1 fusion.144
  306.6 1.1 maximum_multiply_fusion
  (87 shorter events, 6.9 us)
Async XLA Ops:
  6.5 71.0 %all-gather.4.cloned.1.call-start = ((), (), s32[]{:S(2)}) async-start(), calls=%async_computation.2 | async-start | bytes 5570560 | tf_op jit(solution)/shard_map/all_gather | solution.py:58
  14.5 10.2 %copy-start.15 = (s32[5,8]{1,0:T(8,128)S(1)}, s32[5,8]{1,0:T(8,128)}, u32[]{:S(2)}) copy-start(s32[5,8]{1,0:T(8,128)} %param.11) | copy-start | bytes 484
  20.0 0.7 copy-start.7
  20.8 163.5 %all-gather.6.cloned.1.call-start = ((), (), s32[]{:S(2)}) async-start(), calls=%async_computation.3 | async-start | bytes 8912896 | tf_op jit(solution)/shard_map/all_gather | solution.py:69
  88.0 2.3 copy-start.3
  88.0 2.3 copy-start.4
  88.0 2.3 copy-start.6
  90.3 1.6 copy-start.14
  91.0 1.7 copy-start.13
  92.0 3.9 %copy-start.1 = (bf16[512,512]{0,1:T(8,128)(2,1)S(1)}, bf16[512,512]{0,1:T(8,128)(2,1)}, u32[]{:S(2)}) copy-start(bf16[512,512]{0,1:T(8,128)(2,1)} %get-tuple-element.29) | copy-start | bytes 1572868
  92.0 3.9 %copy-start.2 = (bf16[512,512]{0,1:T(8,128)(2,1)S(1)}, bf16[512,512]{0,1:T(8,128)(2,1)}, u32[]{:S(2)}) copy-start(bf16[512,512]{0,1:T(8,128)(2,1)} %get-tuple-element.30) | copy-start | bytes 1572868
  96.0 1.6 copy-start.12
  103.8 4.3 %copy-start.11 = (pred[8]{0:T(512)(128)(4,1)S(1)}, pred[8]{0:T(512)(128)(4,1)}, u32[]{:S(2)}) copy-start(pred[8]{0:T(512)(128)(4,1)} %get-tuple-element.69) | copy-start | bytes 28
  107.5 1.4 copy-start
  107.6 1.4 copy-start.5
  108.9 11.9 %copy-start.10 = (bf16[1,2,2,32,512]{4,3,2,1,0:T(8,128)(2,1)S(1)}, bf16[1,2,2,32,512]{4,3,2,1,0:T(8,128)(2,1)}, u32[]{:S(2)}) copy-start(bf16[1,2,2,32,512]{4,3,2,1,0:T(8,128)(2,1)} %get-tuple-element.43) | copy-start | bytes 393220
  108.9 11.9 %copy-start.9 = (bf16[1,2,2,32,512]{4,3,2,1,0:T(8,128)(2,1)S(1)}, bf16[1,2,2,32,512]{4,3,2,1,0:T(8,128)(2,1)}, u32[]{:S(2)}) copy-start(bf16[1,2,2,32,512]{4,3,2,1,0:T(8,128)(2,1)} %get-tuple-element.42) | copy-start | bytes 393220
  111.2 136.0 %all-gather.8.cloned.1.call-start = ((), (), s32[]{:S(2)}) async-start(), calls=%async_computation.4 | async-start | bytes 5570560 | tf_op jit(solution)/shard_map/all_gather | solution.py:58
  120.9 0.7 copy-start.8
  184.2 5.2 %copy-start.16 = (bf16[2,512,4096]{2,1,0:T(8,128)(2,1)S(1)}, bf16[2,512,4096]{2,1,0:T(8,128)(2,1)}, u32[]{:S(2)}) copy-start(bf16[2,512,4096]{2,1,0:T(8,128)(2,1)} %all-gather.6.cloned.1.call-done) | copy-start | bytes 25165828
  189.5 3.0 copy-start.17
  196.5 56.4 %all-to-all-start = ((bf16[2,512,256]{2,0,1:T(2,128)(2,1)}), bf16[2,512,256]{2,0,1:T(2,128)(2,1)S(1)}, u32[]{:S(2)}, u32[]{:S(2)}) async-start(bf16[2,512,256]{2,0,1:T(2,128)(2,1)} %copy.68), calls=%async_computation | async-start | bytes 1048576 | tf_op jit(solution)/shard_map/all_to_all | solution.py:72
  277.6 19.0 %all-to-all-start.1 = ((bf16[16,2,8192]{2,1,0:T(2,128)(2,1)}), bf16[16,2,8192]{2,1,0:T(2,128)(2,1)}, u32[]{:S(2)}, u32[]{:S(2)}) async-start(bf16[16,2,8192]{2,1,0:T(2,128)(2,1)} %reshape.198), calls=%async_computation.1 | async-start | bytes 1048576 | tf_op jit(solution)/shard_map/all_to_all | solution.py:75
Sparse Core Ops, SparseCore 0:
  20.9 56.6 all-gather.3
  111.3 72.8 all-gather.5
  186.4 60.7 all-gather.7

commit v2 on v1

--- a/solution.py
+++ b/solution.py
@@ -1,6 +1,10 @@
+import functools
+
 import jax
 import jax.numpy as jnp
 from jax import lax
+from jax.experimental import pallas as pl
+from jax.experimental.pallas import tpu as pltpu
 from jax.sharding import PartitionSpec as P
 
 
@@ -46,7 +50,273 @@
     return jnp.stack([real_part, imag_part])
 
 
-def shards(left_stem, right_stem, branches, slice_bits, perms):
+def ring_place(index, reach):
+    chip = index // 2
+    column, level = chip % 2, chip // 2
+    return level + column * (2 * reach - 1 - 2 * level)
+
+
+def ring_device(place, core, reach):
+    place = lax.rem(place + 4 * reach, 2 * reach)
+    column = place // reach
+    level = place + column * (2 * reach - 1 - 2 * place)
+    return (level * 2 + column) * 2 + core
+
+
+class Gather:
+    def __init__(self, buf, send_sems, recv_sems, reach):
+        self.buf, self.send_sems, self.recv_sems, self.reach = buf, send_sems, recv_sems, reach
+        self.me = lax.axis_index("row")
+        self.core = self.me % 2
+        self.place = ring_place(self.me, reach)
+        self.right = ring_device(self.place + 1, self.core, reach)
+        self.left = ring_device(self.place - 1, self.core, reach)
+        self.twin = self.me + 1 - 2 * self.core
+
+    def origin(self, side, distance, core):
+        step = -distance if side == 0 else distance
+        return ring_device(self.place + step, core, self.reach)
+
+    def copy(self, origin, half, slot, target):
+        ref = self.buf.at[origin] if half is None else self.buf.at[origin, half]
+        return pltpu.make_async_remote_copy(
+            src_ref=ref, dst_ref=ref,
+            send_sem=self.send_sems.at[slot], recv_sem=self.recv_sems.at[slot],
+            device_id={"row": target}, device_id_type=pl.DeviceIdType.MESH,
+        )
+
+    def ring_copy(self, side, distance):
+        half = side if distance == self.reach else None
+        origin = self.origin(side, distance - 1, self.core)
+        target = self.right if side == 0 else self.left
+        return self.copy(origin, half, side * self.reach + distance - 1, target)
+
+    def ring_arrival(self, side, distance):
+        half = side if distance == self.reach else None
+        origin = self.origin(side, distance, self.core)
+        target = self.right if side == 0 else self.left
+        return self.copy(origin, half, side * self.reach + distance - 1, target)
+
+    def twin_copy(self, side, distance, core):
+        half = side if distance == self.reach else None
+        origin = self.origin(side, distance, core)
+        slot = 2 * self.reach if distance == 0 else 2 * self.reach + side * self.reach + distance
+        return self.copy(origin, half, slot, self.twin)
+
+    def start(self):
+        self.ring_copy(0, 1).start()
+        self.ring_copy(1, 1).start()
+        self.twin_copy(0, 0, self.core).start()
+
+    def step(self, distance):
+        for side in (0, 1):
+            self.ring_arrival(side, distance).wait_recv()
+            if distance < self.reach:
+                self.ring_copy(side, distance + 1).start()
+            self.twin_copy(side, distance, self.core).start()
+
+    def wait_twin(self, distance):
+        for side in (0, 1) if distance else (0,):
+            self.twin_copy(side, distance, 1 - self.core).wait_recv()
+
+    def finish(self):
+        for distance in range(1, self.reach + 1):
+            for side in (0, 1):
+                self.ring_copy(side, distance).wait_send()
+                self.twin_copy(side, distance, self.core).wait_send()
+        self.twin_copy(0, 0, self.core).wait_send()
+
+
+def cross(a_real, a_imag, w_real, w_imag, transposed):
+    dims = (((1,), (1 if transposed else 0,)), ((), ()))
+
+    def dot(a, w):
+        return lax.dot_general(a, w, dims, preferred_element_type=jnp.float32)
+
+    return dot(a_real, w_real) - dot(a_imag, w_imag), dot(a_real, w_imag) + dot(a_imag, w_real)
+
+
+def core_kernel(n, x_hbm, right_ref, branch_ref, bits_ref, order_ref, tt_ref, q_ref,
+                pbuf, qbuf, dbuf, xbuf, fbuf, sbuf, acc, x_sem, send_sems, recv_sems):
+    reach = n // 4
+    me = lax.axis_index("row")
+    sweeps = pbuf.shape[2]
+    groups, rows, width = fbuf.shape[1:]
+    bundle = width // groups
+    x_copy = pltpu.make_async_copy(x_hbm, xbuf, x_sem)
+    x_copy.start()
+    gathers = [
+        Gather(buf, send_sems.at[i], recv_sems.at[i], reach)
+        for i, buf in enumerate((pbuf, qbuf, dbuf))
+    ]
+    gp, gq, gd = gathers
+
+    barrier = pltpu.get_barrier_semaphore()
+    for other in (gp.right, gp.left, gp.twin):
+        pl.semaphore_signal(barrier, inc=1, device_id={"row": other}, device_id_type=pl.DeviceIdType.MESH)
+    for s in range(sweeps):
+        for plane in (0, 1):
+            pbuf[me, plane, s] = branch_ref[2 * s, bits_ref[2 * s], plane]
+            qbuf[me, plane, s] = branch_ref[2 * s + 1, bits_ref[2 * s + 1], plane]
+    pl.semaphore_wait(barrier, 3)
+    gp.start()
+
+    at = lax.broadcasted_iota(jnp.int32, (width, width), 0)
+    to = lax.broadcasted_iota(jnp.int32, (width, width), 1)
+    turn = (at == (to % bundle) * groups + to // bundle).astype(jnp.bfloat16)
+
+    def turned_rows(w):
+        out = lax.dot_general(turn, w, (((0,), (0,)), ((), ())), preferred_element_type=jnp.float32)
+        return out.astype(jnp.bfloat16)
+
+    def turned_cols(w):
+        return jnp.dot(w, turn, preferred_element_type=jnp.float32).astype(jnp.bfloat16)
+
+    def exchange(index):
+        low = lax.broadcasted_iota(jnp.int32, (rows, 2 * bundle), 1) < bundle
+        for plane in (0, 1):
+            for u in range(groups // 2):
+                first = fbuf[plane, index(2 * u)]
+                second = fbuf[plane, index(2 * u + 1)]
+                there = pl.ds(2 * bundle * u, 2 * bundle)
+                for t in range(groups // 2):
+                    here = slice(2 * bundle * t, 2 * bundle * (t + 1))
+                    a, b = first[:, here], second[:, here]
+                    even = jnp.where(low, a, pltpu.roll(b, bundle, 1))
+                    odd = jnp.where(low, pltpu.roll(a, bundle, 1), b)
+                    sbuf[plane, 2 * t, :, there] = even.astype(jnp.bfloat16)
+                    sbuf[plane, 2 * t + 1, :, there] = odd.astype(jnp.bfloat16)
+
+    def operand(index):
+        return [
+            jnp.concatenate([sbuf[plane, index(g)] for g in range(groups)], axis=0) for plane in (0, 1)
+        ]
+
+    def branch(s):
+        return [pbuf[:, plane, s].reshape(width, width) for plane in (0, 1)]
+
+    def keep(pair, ref):
+        for plane in (0, 1):
+            ref[plane] = pair[plane].reshape(groups, rows, width).astype(ref.dtype)
+
+    for plane in (0, 1):
+        for g in range(groups):
+            block = right_ref[plane, :, pl.ds(g * width, width)]
+            fbuf[plane, g] = jnp.dot(block, turn, preferred_element_type=jnp.float32)
+    exchange(lambda i: i)
+
+    for d in range(1, reach):
+        gp.step(d)
+    gq.start()
+    gp.step(reach)
+    for d in range(reach + 1):
+        gp.wait_twin(d)
+
+    keep(cross(*operand(lambda g: g), *branch(3), False), fbuf)
+    exchange(lambda i: i)
+    w4 = [turned_rows(w) for w in branch(4)]
+    keep(cross(*operand(lambda g: order_ref[3, g]), *w4, False), sbuf)
+    gq.step(1)
+    w2 = [turned_rows(w) for w in branch(2)]
+    keep(cross(*operand(lambda g: order_ref[4, order_ref[2, g]]), *w2, True), fbuf)
+    exchange(lambda i: order_ref[1, i])
+    gq.step(2)
+    keep(cross(*operand(lambda g: g), *branch(1), True), fbuf)
+    exchange(lambda i: i)
+    w0 = [turned_cols(w) for w in branch(0)]
+    last = cross(*operand(lambda g: order_ref[0, g]), *w0, True)
+    for plane in (0, 1):
+        for g in range(groups):
+            part = last[plane][g * rows : (g + 1) * rows]
+            dbuf[me, plane, :, pl.ds(g * width, width)] = part.astype(jnp.bfloat16)
+    gq.step(3)
+    gd.start()
+    gq.step(reach)
+    x_copy.wait()
+
+    def join(origins):
+        high = len(origins) * rows
+        acc[...] = jnp.zeros_like(acc)
+
+        @pl.loop(0, groups)
+        def _(g):
+            cols = pl.ds(pl.multiple_of(g * width, width), width)
+            a = jnp.concatenate(
+                [dbuf[o, plane, :, cols] for plane in (0, 1) for o in origins], axis=0
+            )
+            dims = (((1,), (1,)), ((), ()))
+            for plane in (0, 1):
+                acc[plane, : 2 * high] += lax.dot_general(
+                    a, xbuf[plane, :, cols], dims, preferred_element_type=jnp.float32
+                )
+
+        for i, o in enumerate(origins):
+            real = slice(i * rows, (i + 1) * rows)
+            imag = slice(high + i * rows, high + (i + 1) * rows)
+            tt_ref[o, 0] = (acc[0, real] - acc[1, imag]).astype(tt_ref.dtype)
+            tt_ref[o, 1] = (acc[1, real] + acc[0, imag]).astype(tt_ref.dtype)
+
+    gd.wait_twin(0)
+    join([me, gd.twin])
+    for d in range(1, reach):
+        gd.step(d)
+        gd.wait_twin(d)
+        join([gd.origin(side, d, core) for side in (0, 1) for core in (0, 1)])
+    for d in range(reach + 1):
+        gq.wait_twin(d)
+    q_ref[...] = qbuf[...]
+    gd.step(reach)
+    gd.wait_twin(reach)
+    join([gd.origin(0, reach, core) for core in (0, 1)])
+    for gather in gathers:
+        gather.finish()
+
+
+def fused(n, left_stem, right_stem, branches, bits, order):
+    planes, tall, cols = left_stem.shape
+    rows = right_stem.shape[1]
+    part, width = branches.shape[3:]
+    sweeps, groups = order.shape
+    vmem = pl.BlockSpec(memory_space=pltpu.VMEM)
+    smem = pl.BlockSpec(memory_space=pltpu.SMEM)
+    bf16 = jnp.bfloat16
+    slots = 4 * (n // 4) + 1
+    return pl.pallas_call(
+        functools.partial(core_kernel, n),
+        out_shape=(
+            jax.ShapeDtypeStruct((n, planes, rows, tall), bf16),
+            jax.ShapeDtypeStruct((n, planes, sweeps, part, width), bf16),
+        ),
+        in_specs=[pl.BlockSpec(memory_space=pl.ANY), vmem, vmem, smem, smem],
+        out_specs=(vmem, vmem),
+        scratch_shapes=[
+            pltpu.VMEM((n, planes, sweeps, part, width), bf16),
+            pltpu.VMEM((n, planes, sweeps, part, width), bf16),
+            pltpu.VMEM((n, planes, rows, cols), bf16),
+            pltpu.VMEM((planes, tall, cols), bf16),
+            pltpu.VMEM((planes, groups, rows, width), jnp.float32),
+            pltpu.VMEM((planes, groups, rows, width), bf16),
+            pltpu.VMEM((planes, 8 * rows, tall), jnp.float32),
+            pltpu.SemaphoreType.DMA,
+            pltpu.SemaphoreType.DMA((3, slots)),
+            pltpu.SemaphoreType.DMA((3, slots)),
+        ],
+        compiler_params=pltpu.CompilerParams(
+            collective_id=0, has_side_effects=True, vmem_limit_bytes=58 * 2**20
+        ),
+    )(left_stem, right_stem, branches, bits, order)
+
+
+def fits(n, right_stem, branches, order):
+    part, width = branches.shape[3:]
+    groups = order.shape[1]
+    return (
+        n % 8 == 0 and n // 4 == 4 and part % 16 == 0 and right_stem.shape[1] % 16 == 0
+        and width // groups == 64 and n * right_stem.shape[1] == width and order.shape[0] == 5
+    )
+
+
+def shards(n, left_stem, right_stem, branches, slice_bits, perms):
     left_sweeps = 3
     sweeps = perms.shape[0]
 
@@ -57,18 +327,27 @@
         stacked = jnp.stack([own(index) for index in indices])
         return lax.all_gather(stacked, "row", axis=2, tiled=True)
 
-    col_mats = fetch([2 * s for s in range(sweeps)])
-    row_mats = fetch([2 * s + 1 for s in range(sweeps)])
-
-    stem = right_stem
-    for s in range(left_sweeps, sweeps):
-        stem = permute(mix(stem, col_mats[s], s % 2 == 1, False), perms[s])
-    for s in reversed(range(left_sweeps)):
-        stem = permute(stem, jnp.argsort(perms[s]))
-        stem = mix(stem, col_mats[s], s % 2 == 1, True)
-    gathered = lax.all_gather(stem, "row", axis=1, tiled=True)
-
-    joined = contract(gathered, left_stem, ((1,), (1,))).astype(jnp.bfloat16)
+    if fits(n, right_stem, branches, perms):
+        numbers = jnp.arange(perms.shape[1], dtype=jnp.int32)
+        hit = (perms[:, None, :] == numbers[None, :, None]).astype(jnp.int32)
+        undo = jnp.sum(hit * numbers, axis=2)
+        order = jnp.concatenate([undo[:left_sweeps], perms[left_sweeps:]])
+        blocks, parts = fused(n, left_stem, right_stem, branches, slice_bits, order)
+        joined = blocks.transpose(1, 0, 2, 3).reshape(2, -1, left_stem.shape[1])
+        width = branches.shape[-1]
+        row_mats = parts.transpose(2, 1, 0, 3, 4).reshape(sweeps, 2, width, width)
+    else:
+        row_mats = fetch([2 * s + 1 for s in range(sweeps)])
+        col_mats = fetch([2 * s for s in range(sweeps)])
+        stem = right_stem
+        for s in range(left_sweeps, sweeps):
+            stem = permute(mix(stem, col_mats[s], s % 2 == 1, False), perms[s])
+        for s in reversed(range(left_sweeps)):
+            stem = permute(stem, jnp.argsort(perms[s]))
+            stem = mix(stem, col_mats[s], s % 2 == 1, True)
+        gathered = lax.all_gather(stem, "row", axis=1, tiled=True)
+        joined = contract(gathered, left_stem, ((1,), (1,))).astype(jnp.bfloat16)
+
     spread = lax.all_to_all(joined, "row", split_axis=1, concat_axis=2, tiled=True)
     for s in range(left_sweeps):
         spread = mix(spread, row_mats[s], s % 2 == 1, True)
@@ -90,4 +369,4 @@
         P("cuts", None),
     )
     out_specs = P(None, ("cuts", "row"), None)
-    return jax.shard_map(shards, mesh=mesh, in_specs=in_specs, out_specs=out_specs, check_vma=False)
+    return jax.shard_map(functools.partial(shards, mesh.shape["row"]), mesh=mesh, in_specs=in_specs, out_specs=out_specs, check_vma=False)

time: 317 us -> 191 us (0.60)
  waiting for transfers between devices: 163 us -> 15.9 us
  Pallas kernels: 0 us -> 111 us
  between operations: 32.9 us -> 0.2 us
  local copies, waits for them, and re-layouts: 60.7 us -> 32.2 us
  matrix products: 32.4 us -> 15.2 us
  other arithmetic: 14.4 us -> 4.65 us
    all_gather x3 -> x0, waiting for transfers between devices: 156 us -> none  [the longest x2 93.4 us: fetch(): return lax.all_gather(stacked, 'row', axis=2, tiled=True)]
    pallas_call x0 -> x1, Pallas kernels: none -> 111 us  [fused(): pl.pallas_call(functools.partial(core_kernel, n), out_shape=(jax.ShapeDty...]
    dot_general x12 -> x8, matrix products: 17.8 us -> 6.22 us  [dot(): lax.dot_general(a, b, (dims, ((), ())), preferred_element_type=jnp.float32)]
    unnamed x55 -> x17, local copies, waits for them, and re-layouts: 20.8 us -> 12.4 us
    transpose x3 -> x1, local copies, waits for them, and re-layouts: 9.22 us -> 1.08 us  [shards(): joined = blocks.transpose(1, 0, 2, 3).reshape(2, -1, left_stem.shape[1])]
    all_to_all x1, waiting for transfers between devices: 0.01 us -> 7.05 us  [shards(): lax.all_to_all(joined, 'row', split_axis=1, concat_axis=2, tiled=True)]
    dot_general x8 -> x3, matrix products: 14.6 us -> 9.01 us  [mix(): jnp.dot(flat, packed(matrix, transposed), preferred_element_type=jnp.floa...]
    neg x3 -> x2, other arithmetic: 7.2 us -> 2.1 us  [packed(): bottom = jnp.concatenate([-imag, real], axis=1)]
  transfers between devices with their start and end apart: 5 -> 2, of which waited for: 4 -> 2; matrix products, arithmetic and copies ran while one was open for 10% -> 6% of each run, Pallas kernels for 0% -> 0%
where the time goes in v2:
time: 191 us; the launch traced here: 188 us
  Pallas kernels  111 us (58%)
  local copies, waits for them, and re-layouts  32.2 us (17%)
  waiting for transfers between devices  15.9 us (8%)
  matrix products  15.2 us (8%)
  starting transfers between devices  9.57 us (5%)
  other arithmetic  4.65 us (2%)
    pallas_call x1, Pallas kernels, fused(): pl.pallas_call(functools.partial(core_kernel, n), out_shape=(jax.ShapeDty...  111 us
    unnamed x17, local copies, waits for them, and re-layouts  12.4 us
    dot_general x3, matrix products, mix(): jnp.dot(flat, packed(matrix, transposed), preferred_element_type=jnp.floa...  9.01 us
    all_to_all x1, waiting for transfers between devices, shards(): lax.all_to_all(spread, 'row', split_axis=2, concat_axis=1, tiled=True)  8.84 us
    all_to_all x1, waiting for transfers between devices, shards(): lax.all_to_all(joined, 'row', split_axis=1, concat_axis=2, tiled=True)  7.05 us
    dot_general x8, matrix products, dot(): lax.dot_general(a, b, (dims, ((), ())), preferred_element_type=jnp.float32)  6.22 us
    slice x4, local copies, waits for them, and re-layouts, contract(): real_part = dot(left[0], right[0]) - dot(left[1], right[1])  5.52 us
    all_to_all x1, starting transfers between devices, shards(): lax.all_to_all(spread, 'row', split_axis=2, concat_axis=1, tiled=True)  5.12 us
  transfers between devices with their start and end apart: 2, of which 2 were waited for; matrix products, arithmetic and copies ran while one was open for 6% of the time, Pallas kernels for 0%

profile of v2, /device:TPU:13, one launch (start us, length us, event | category | flops | bytes accessed | tf_op | source)
XLA Modules:
  0.0 188.4 jit_solution(15233420415955370913)
XLA Ops:
  0.0 0.7 slice.85
  0.7 0.9 select_reduce_fusion
  1.6 0.6 pad_add_fusion.order_ref
  2.2 110.7 %shard_map.55 = (bf16[16,2,32,256]{3,2,1,0:T(8,128)(2,1)}, bf16[16,2,5,32,512]{4,3,2,1,0:T(8,128)(2,1)}) custom-call(bf16[2,256,4096]{2,1,0:T(8,128)(2,1)} %x_hbm.1, bf16[2,32,4096]{2,1,0:T(8,128)(2,1)} %right_ref.1, bf16[10,2,2,32,512]{4,3,2,1,0:T(8,128)(2,1)} %branch_ref.1, s32[10]{0:T(128)} %bits_ref.1, s32[5,8]{1,0:T(8,128)} %pad_add_fusion.order_ref), custom_call_target="tpu_custom_call" | custom-call | tf_op jit(solution)/shard_map/pallas_call | solution.py:284
  112.8 1.1 copy.35
  113.9 1.3 copy.36
  115.3 4.4 %all-to-all-start = ((bf16[2,512,256]{2,0,1:T(2,128)(2,1)}), bf16[2,512,256]{2,0,1:T(2,128)(2,1)S(1)}, u32[]{:S(2)}, u32[]{:S(2)}) async-start(bf16[2,512,256]{2,0,1:T(2,128)(2,1)} %copy.36), calls=%async_computation | async-start | bytes 1048576 | tf_op jit(solution)/shard_map/all_to_all | solution.py:351
  119.7 4.3 %fusion.40 = (bf16[1,1,16,32,512]{4,3,0,1,2:T(8,128)(2,1)}, bf16[1,1,16,32,512]{4,3,0,1,2:T(8,128)(2,1)S(1)}, bf16[1,1,16,32,512]{4,3,0,1,2:T(8,128)(2,1)S(1)}, ...) fusion(bf16[5,2,16,32,512]{4,3,0,1,2:T(8,128)(2,1)} %bitcast.95), kind=kLoop, calls=%fused_computation.47 | loop fusion | bytes 10485760 | tf_op jit(solution)/shard_map/slice | solution.py:48
  124.0 0.0 copy-start.4
  124.0 0.0 copy-start.5
  124.0 0.0 copy-start.1
  124.0 1.0 bitcast_negate_fusion.2
  125.0 0.0 copy-done.4
  125.0 0.1 copy-done.5
  125.1 1.1 bitcast_negate_fusion
  126.3 7.1 %all-to-all-done = bf16[2,512,256]{2,0,1:T(2,128)(2,1)S(1)} async-done(((bf16[2,512,256]{2,0,1:T(2,128)(2,1)}), bf16[2,512,256]{2,0,1:T(2,128)(2,1)S(1)}, u32[]{:S(2)}, u32[]{:S(2)}) %all-to-all-start) | async-done | bytes 524320 | tf_op jit(solution)/shard_map/all_to_all | solution.py:351
  133.3 0.3 copy.56
  133.6 0.2 reshape.67
  133.8 0.5 copy.55
  134.3 0.1 copy.48
  134.4 2.6 %fusion.30 = bf16[256,1024]{1,0:T(8,128)(2,1)} fusion(bf16[256,1024]{1,0:T(8,128)(2,1)S(1)} %bitcast.124, bf16[512,512]{0,1:T(8,128)(2,1)S(1)} %bitcast.118, bf16[512,512]{0,1:T(8,128)(2,1)} %bitcast_negate_fusion.2, bf16[512,512]{0,1:T(8,128)(2,1)S(1)} %bitcast.108), kind=kOutput, calls=%fused_computation.28 | convolution fusion | flops 545521664 | bytes 2621440 | tf_op jit(solution)/shard_map/dot_general | solution.py:30
  137.0 2.0 %copy.39 = bf16[32,8,2,512]{0,3,1,2:T(8,128)(2,1)S(1)} copy(bf16[32,8,2,512]{3,1,2,0:T(8,128)(2,1)} %bitcast.120) | data formatting | bytes 1048576 | tf_op jit(solution)/shard_map/reshape | solution.py:31
  139.0 2.6 %copy.49 = bf16[32,8,2,512]{3,1,2,0:T(8,128)(2,1)} copy(bf16[32,8,2,512]{0,1,3,2:T(8,128)(2,1)S(1)} %bitcast.91) | data formatting | bytes 1048576
  141.6 3.2 %fusion.27 = bf16[256,1024]{1,0:T(8,128)(2,1)} fusion(bf16[256,1024]{1,0:T(8,128)(2,1)} %bitcast.121, bf16[512,512]{0,1:T(8,128)(2,1)} %bitcast.117, bf16[512,512]{0,1:T(8,128)(2,1)} %get-tuple-element.22, bf16[512,512]{0,1:T(8,128)(2,1)} %bitcast.111), kind=kOutput, calls=%fused_computation.27 | convolution fusion | flops 545521664 | bytes 2621440 | tf_op jit(solution)/shard_map/dot_general | solution.py:30
  144.8 2.7 %copy.41 = bf16[32,8,2,512]{0,1,3,2:T(8,128)(2,1)S(1)} copy(bf16[32,8,2,512]{3,1,2,0:T(8,128)(2,1)} %bitcast.122) | data formatting | bytes 1048576 | tf_op jit(solution)/shard_map/reshape | solution.py:31
  147.6 1.8 copy.50
  149.4 3.2 %fusion.24 = bf16[256,1024]{1,0:T(8,128)(2,1)} fusion(bf16[256,1024]{1,0:T(8,128)(2,1)} %bitcast.119, bf16[512,512]{0,1:T(8,128)(2,1)} %bitcast.116, bf16[512,512]{0,1:T(8,128)(2,1)} %get-tuple-element.21, bf16[512,512]{0,1:T(8,128)(2,1)} %bitcast.110), kind=kOutput, calls=%fused_computation.26 | convolution fusion | flops 545521664 | bytes 2621440 | tf_op jit(solution)/shard_map/dot_general | solution.py:30
  152.6 3.3 %copy.43 = bf16[2,32,8,512]{1,0,3,2:T(2,128)(2,1)S(1)} copy(bf16[2,32,8,512]{3,2,0,1:T(8,128)(2,1)} %bitcast.123) | data formatting | bytes 1048576 | tf_op jit(solution)/shard_map/transpose | solution.py:34
  155.9 2.7 %reshape.75 = bf16[16,2,8192]{2,1,0:T(2,128)(2,1)} reshape(bf16[4096,2,32]{2,1,0:T(2,128)(2,1)S(1)} %bitcast.93) | data formatting | bytes 1048576
  158.5 0.0 copy-start.3
  158.5 5.1 %all-to-all-start.1 = ((bf16[16,2,8192]{2,1,0:T(2,128)(2,1)}), bf16[16,2,8192]{2,1,0:T(2,128)(2,1)}, u32[]{:S(2)}, u32[]{:S(2)}) async-start(bf16[16,2,8192]{2,1,0:T(2,128)(2,1)} %reshape.75), calls=%async_computation.1 | async-start | bytes 1048576 | tf_op jit(solution)/shard_map/all_to_all | solution.py:354
  163.6 0.0 copy-done.1
  163.6 1.5 fusion.44
  165.1 0.0 copy-start.2
  165.1 1.7 fusion.42
  166.8 0.0 copy-done.3
  166.8 0.4 fusion.34
  167.3 0.0 copy-done.2
  167.3 1.2 fusion.33
  168.5 0.0 copy-start
  168.5 8.8 %all-to-all-done.1 = bf16[16,2,8192]{2,1,0:T(2,128)(2,1)} async-done(((bf16[16,2,8192]{2,1,0:T(2,128)(2,1)}), bf16[16,2,8192]{2,1,0:T(2,128)(2,1)}, u32[]{:S(2)}, u32[]{:S(2)}) %all-to-all-start.1) | async-done | bytes 524320 | tf_op jit(solution)/shard_map/all_to_all | solution.py:354
  177.4 5.1 %reshape.76 = bf16[4096,2,32]{2,1,0:T(2,128)(2,1)S(1)} reshape(bf16[16,2,8192]{2,1,0:T(2,128)(2,1)} %all-to-all-done.1) | data formatting | bytes 1048576
  182.5 2.2 %copy.47 = bf16[2,32,16,256]{3,2,1,0:T(8,128)(2,1)} copy(bf16[2,32,16,256]{1,0,3,2:T(2,128)(2,1)S(1)} %bitcast.94) | data formatting | bytes 1048576 | tf_op jit(solution)/shard_map/all_to_all | solution.py:354
  184.6 1.1 fusion.41
  185.7 0.1 copy.46
  185.8 0.1 copy.45
  185.9 0.3 fusion.45
  186.2 0.0 copy-done
  186.2 0.3 fusion.43
  186.6 0.4 fusion.35
  186.9 0.3 fusion.36
  187.3 1.1 maximum_multiply_fusion
  (1 shorter events, 0.0 us)
Async XLA Ops:
  115.3 18.1 %all-to-all-start = ((bf16[2,512,256]{2,0,1:T(2,128)(2,1)}), bf16[2,512,256]{2,0,1:T(2,128)(2,1)S(1)}, u32[]{:S(2)}, u32[]{:S(2)}) async-start(bf16[2,512,256]{2,0,1:T(2,128)(2,1)} %copy.36), calls=%async_computation | async-start | bytes 1048576 | tf_op jit(solution)/shard_map/all_to_all | solution.py:351
  124.0 1.0 copy-start.4
  124.0 1.1 copy-start.5
  124.0 39.6 %copy-start.1 = (bf16[1,1,16,32,512]{4,3,0,1,2:T(8,128)(2,1)}, bf16[1,1,16,32,512]{4,3,0,1,2:T(8,128)(2,1)S(1)}, u32[]{:S(2)}) copy-start(bf16[1,1,16,32,512]{4,3,0,1,2:T(8,128)(2,1)S(1)} %get-tuple-element.10) | copy-start | bytes 1572868
  158.5 8.3 %copy-start.3 = (bf16[1,1,16,32,512]{4,3,0,1,2:T(8,128)(2,1)S(1)}, bf16[1,1,16,32,512]{4,3,0,1,2:T(8,128)(2,1)}, u32[]{:S(2)}) copy-start(bf16[1,1,16,32,512]{4,3,0,1,2:T(8,128)(2,1)} %get-tuple-element.9) | copy-start | bytes 1572868
  158.5 18.8 %all-to-all-start.1 = ((bf16[16,2,8192]{2,1,0:T(2,128)(2,1)}), bf16[16,2,8192]{2,1,0:T(2,128)(2,1)}, u32[]{:S(2)}, u32[]{:S(2)}) async-start(bf16[16,2,8192]{2,1,0:T(2,128)(2,1)} %reshape.75), calls=%async_computation.1 | async-start | bytes 1048576 | tf_op jit(solution)/shard_map/all_to_all | solution.py:354
  165.1 2.2 %copy-start.2 = (bf16[1,1,16,32,512]{4,3,0,1,2:T(8,128)(2,1)S(1)}, bf16[1,1,16,32,512]{4,3,0,1,2:T(8,128)(2,1)}, u32[]{:S(2)}) copy-start(bf16[1,1,16,32,512]{4,3,0,1,2:T(8,128)(2,1)} %copy-done.1) | copy-start | bytes 1572868
  168.5 17.7 %copy-start = (bf16[512,512]{1,0:T(8,128)(2,1)S(1)}, bf16[512,512]{1,0:T(8,128)(2,1)}, u32[]{:S(2)}) copy-start(bf16[512,512]{1,0:T(8,128)(2,1)} %fusion.33) | copy-start | bytes 1572868

commit v3 on v2

--- a/solution.py
+++ b/solution.py
@@ -136,8 +136,9 @@
     return dot(a_real, w_real) - dot(a_imag, w_imag), dot(a_real, w_imag) + dot(a_imag, w_real)
 
 
-def core_kernel(n, x_hbm, right_ref, branch_ref, bits_ref, order_ref, tt_ref, q_ref,
-                pbuf, qbuf, dbuf, xbuf, fbuf, sbuf, acc, x_sem, send_sems, recv_sems):
+def core_kernel(n, scale, x_hbm, right_ref, branch_ref, bits_ref, order_ref, out_ref,
+                pbuf, qbuf, dbuf, xbuf, fbuf, sbuf, acc, near, far, wbuf, x_sem,
+                send_sems, recv_sems, near_sems, far_sems):
     reach = n // 4
     me = lax.axis_index("row")
     sweeps = pbuf.shape[2]
@@ -152,13 +153,18 @@
     gp, gq, gd = gathers
 
     barrier = pltpu.get_barrier_semaphore()
-    for other in (gp.right, gp.left, gp.twin):
-        pl.semaphore_signal(barrier, inc=1, device_id={"row": other}, device_id_type=pl.DeviceIdType.MESH)
+
+    @pl.loop(1, n)
+    def _(i):
+        pl.semaphore_signal(
+            barrier, inc=1, device_id={"row": lax.rem(me + i, n)}, device_id_type=pl.DeviceIdType.MESH
+        )
+
     for s in range(sweeps):
         for plane in (0, 1):
             pbuf[me, plane, s] = branch_ref[2 * s, bits_ref[2 * s], plane]
             qbuf[me, plane, s] = branch_ref[2 * s + 1, bits_ref[2 * s + 1], plane]
-    pl.semaphore_wait(barrier, 3)
+    pl.semaphore_wait(barrier, n - 1)
     gp.start()
 
     at = lax.broadcasted_iota(jnp.int32, (width, width), 0)
@@ -234,7 +240,7 @@
     gq.step(reach)
     x_copy.wait()
 
-    def join(origins):
+    def join(origins, own=False):
         high = len(origins) * rows
         acc[...] = jnp.zeros_like(acc)
 
@@ -253,26 +259,106 @@
         for i, o in enumerate(origins):
             real = slice(i * rows, (i + 1) * rows)
             imag = slice(high + i * rows, high + (i + 1) * rows)
-            tt_ref[o, 0] = (acc[0, real] - acc[1, imag]).astype(tt_ref.dtype)
-            tt_ref[o, 1] = (acc[1, real] + acc[0, imag]).astype(tt_ref.dtype)
+            near[turn_one, o, 0] = (acc[0, real] - acc[1, imag]).astype(near.dtype)
+            near[turn_one, o, 1] = (acc[1, real] + acc[0, imag]).astype(near.dtype)
+            if not (own and i == 0):
+                trade(turn_one, o, o).start()
+
+    turn_one, turn_two = 0, 1
+
+    def trade(turn_at, target, slot):
+        return pltpu.make_async_remote_copy(
+            src_ref=near.at[turn_at, target], dst_ref=far.at[turn_at, me],
+            send_sem=near_sems.at[turn_at, slot], recv_sem=far_sems.at[turn_at, me],
+            device_id={"row": target}, device_id_type=pl.DeviceIdType.MESH,
+        )
+
+    def arrival(turn_at, source):
+        return pltpu.make_async_remote_copy(
+            src_ref=near.at[turn_at, source], dst_ref=far.at[turn_at, source],
+            send_sem=near_sems.at[turn_at, source], recv_sem=far_sems.at[turn_at, source],
+            device_id={"row": source}, device_id_type=pl.DeviceIdType.MESH,
+        )
+
+    def arrivals(turn_at):
+        far[turn_at, me] = near[turn_at, me]
+
+        @pl.loop(1, n)
+        def _(i):
+            arrival(turn_at, lax.rem(me + i, n)).wait_recv()
 
     gd.wait_twin(0)
-    join([me, gd.twin])
+    join([me, gd.twin], own=True)
     for d in range(1, reach):
         gd.step(d)
         gd.wait_twin(d)
         join([gd.origin(side, d, core) for side in (0, 1) for core in (0, 1)])
     for d in range(reach + 1):
         gq.wait_twin(d)
-    q_ref[...] = qbuf[...]
+
+    def row_factor(s):
+        return [qbuf[:, plane, s].reshape(width, width) for plane in (0, 1)]
+
+    q1 = [turned_rows(w) for w in row_factor(0)]
+    q5 = [turned_cols(w) for w in row_factor(2)]
+    ends = cross(*row_factor(4), *row_factor(3), False)
+    for plane in (0, 1):
+        wbuf[0, plane] = q1[plane]
+        wbuf[1, plane] = q5[plane]
+        wbuf[2, plane] = ends[plane].astype(wbuf.dtype)
     gd.step(reach)
     gd.wait_twin(reach)
     join([gd.origin(0, reach, core) for core in (0, 1)])
+    arrivals(turn_one)
+
+    pieces = n // groups
+    whole = [
+        jnp.concatenate(
+            [
+                jnp.concatenate([far[turn_one, g * pieces + i, plane] for i in range(pieces)], axis=1)
+                for g in range(groups)
+            ],
+            axis=0,
+        )
+        for plane in (0, 1)
+    ]
+    keep(cross(*whole, wbuf[0, 0], wbuf[0, 1], True), fbuf)
+    exchange(lambda i: i)
+    keep(cross(*operand(lambda g: g), *row_factor(1), True), fbuf)
+    exchange(lambda i: i)
+    mixed = cross(*operand(lambda g: g), wbuf[1, 0], wbuf[1, 1], True)
+    tall = width // pieces
+    for plane in (0, 1):
+        for o in range(n):
+            g, i = o // pieces, o % pieces
+            block = mixed[plane][g * rows : (g + 1) * rows, i * tall : (i + 1) * tall]
+            near[turn_two, o, plane] = block.astype(near.dtype)
+
+    @pl.loop(1, n)
+    def _(i):
+        target = lax.rem(me + i, n)
+        trade(turn_two, target, target).start()
+
+    arrivals(turn_two)
+
+    amplitude = cross(
+        *[far[turn_two, :, plane].reshape(width, tall).T for plane in (0, 1)],
+        wbuf[2, 0], wbuf[2, 1], True,
+    )
+    for plane in (0, 1):
+        out_ref[plane] = amplitude[plane] * scale
+
+    for turn_at in (turn_one, turn_two):
+
+        @pl.loop(1, n)
+        def _(i):
+            arrival(turn_at, lax.rem(me + i, n)).wait_send()
+
     for gather in gathers:
         gather.finish()
 
 
-def fused(n, left_stem, right_stem, branches, bits, order):
+def fused(n, scale, left_stem, right_stem, branches, bits, order):
     planes, tall, cols = left_stem.shape
     rows = right_stem.shape[1]
     part, width = branches.shape[3:]
@@ -282,13 +368,10 @@
     bf16 = jnp.bfloat16
     slots = 4 * (n // 4) + 1
     return pl.pallas_call(
-        functools.partial(core_kernel, n),
-        out_shape=(
-            jax.ShapeDtypeStruct((n, planes, rows, tall), bf16),
-            jax.ShapeDtypeStruct((n, planes, sweeps, part, width), bf16),
-        ),
+        functools.partial(core_kernel, n, scale),
+        out_shape=jax.ShapeDtypeStruct((planes, tall, width), jnp.float32),
         in_specs=[pl.BlockSpec(memory_space=pl.ANY), vmem, vmem, smem, smem],
-        out_specs=(vmem, vmem),
+        out_specs=vmem,
         scratch_shapes=[
             pltpu.VMEM((n, planes, sweeps, part, width), bf16),
             pltpu.VMEM((n, planes, sweeps, part, width), bf16),
@@ -297,9 +380,14 @@
             pltpu.VMEM((planes, groups, rows, width), jnp.float32),
             pltpu.VMEM((planes, groups, rows, width), bf16),
             pltpu.VMEM((planes, 8 * rows, tall), jnp.float32),
+            pltpu.VMEM((2, n, planes, rows, tall), bf16),
+            pltpu.VMEM((2, n, planes, rows, tall), bf16),
+            pltpu.VMEM((3, planes, width, width), bf16),
             pltpu.SemaphoreType.DMA,
             pltpu.SemaphoreType.DMA((3, slots)),
             pltpu.SemaphoreType.DMA((3, slots)),
+            pltpu.SemaphoreType.DMA((2, n)),
+            pltpu.SemaphoreType.DMA((2, n)),
         ],
         compiler_params=pltpu.CompilerParams(
             collective_id=0, has_side_effects=True, vmem_limit_bytes=58 * 2**20
@@ -307,12 +395,13 @@
     )(left_stem, right_stem, branches, bits, order)
 
 
-def fits(n, right_stem, branches, order):
+def fits(n, left_stem, right_stem, branches, order):
     part, width = branches.shape[3:]
     groups = order.shape[1]
     return (
         n % 8 == 0 and n // 4 == 4 and part % 16 == 0 and right_stem.shape[1] % 16 == 0
-        and width // groups == 64 and n * right_stem.shape[1] == width and order.shape[0] == 5
+        and width // groups == 64 and n * left_stem.shape[1] == groups * width
+        and n % groups == 0 and n * right_stem.shape[1] == width and order.shape[0] == 5
     )
 
 
@@ -320,33 +409,31 @@
     left_sweeps = 3
     sweeps = perms.shape[0]
 
-    def own(index):
-        return lax.dynamic_index_in_dim(branches[index], slice_bits[index], 0, keepdims=False)
-
-    def fetch(indices):
-        stacked = jnp.stack([own(index) for index in indices])
-        return lax.all_gather(stacked, "row", axis=2, tiled=True)
-
-    if fits(n, right_stem, branches, perms):
+    scale = (2.0 * left_stem.shape[2]) ** (-0.5)
+    if fits(n, left_stem, right_stem, branches, perms):
         numbers = jnp.arange(perms.shape[1], dtype=jnp.int32)
         hit = (perms[:, None, :] == numbers[None, :, None]).astype(jnp.int32)
         undo = jnp.sum(hit * numbers, axis=2)
         order = jnp.concatenate([undo[:left_sweeps], perms[left_sweeps:]])
-        blocks, parts = fused(n, left_stem, right_stem, branches, slice_bits, order)
-        joined = blocks.transpose(1, 0, 2, 3).reshape(2, -1, left_stem.shape[1])
-        width = branches.shape[-1]
-        row_mats = parts.transpose(2, 1, 0, 3, 4).reshape(sweeps, 2, width, width)
-    else:
-        row_mats = fetch([2 * s + 1 for s in range(sweeps)])
-        col_mats = fetch([2 * s for s in range(sweeps)])
-        stem = right_stem
-        for s in range(left_sweeps, sweeps):
-            stem = permute(mix(stem, col_mats[s], s % 2 == 1, False), perms[s])
-        for s in reversed(range(left_sweeps)):
-            stem = permute(stem, jnp.argsort(perms[s]))
-            stem = mix(stem, col_mats[s], s % 2 == 1, True)
-        gathered = lax.all_gather(stem, "row", axis=1, tiled=True)
-        joined = contract(gathered, left_stem, ((1,), (1,))).astype(jnp.bfloat16)
+        return fused(n, scale, left_stem, right_stem, branches, slice_bits, order)
+
+    def own(index):
+        return lax.dynamic_index_in_dim(branches[index], slice_bits[index], 0, keepdims=False)
+
+    def fetch(indices):
+        stacked = jnp.stack([own(index) for index in indices])
+        return lax.all_gather(stacked, "row", axis=2, tiled=True)
+
+    row_mats = fetch([2 * s + 1 for s in range(sweeps)])
+    col_mats = fetch([2 * s for s in range(sweeps)])
+    stem = right_stem
+    for s in range(left_sweeps, sweeps):
+        stem = permute(mix(stem, col_mats[s], s % 2 == 1, False), perms[s])
+    for s in reversed(range(left_sweeps)):
+        stem = permute(stem, jnp.argsort(perms[s]))
+        stem = mix(stem, col_mats[s], s % 2 == 1, True)
+    gathered = lax.all_gather(stem, "row", axis=1, tiled=True)
+    joined = contract(gathered, left_stem, ((1,), (1,))).astype(jnp.bfloat16)
 
     spread = lax.all_to_all(joined, "row", split_axis=1, concat_axis=2, tiled=True)
     for s in range(left_sweeps):
@@ -356,7 +443,6 @@
     right_rows = row_mats[left_sweeps]
     for s in range(left_sweeps + 1, sweeps):
         right_rows = contract(row_mats[s], right_rows, ((1,), (0,))).astype(jnp.bfloat16)
-    scale = (2.0 * left_stem.shape[2]) ** (-0.5)
     return contract(turned, right_rows, ((0,), (1,))) * scale
 
 

time: 191 us -> 139 us (0.73); the launches traced: 188 us -> 139 us
  local copies, waits for them, and re-layouts: 32.2 us -> 2.95 us
  Pallas kernels: 111 us -> 134 us
  waiting for transfers between devices: 15.9 us -> 0 us
  matrix products: 15.2 us -> 0 us
  starting transfers between devices: 9.57 us -> 0 us
  other arithmetic: 4.65 us -> 1.46 us
    pallas_call x1, Pallas kernels: 111 us -> 134 us  [fused(): pl.pallas_call(functools.partial(core_kernel, n, scale), out_shape=jax.Sh...]
    all_to_all x2 -> x0, waiting for transfers between devices: 15.9 us -> none  [the longest x1 8.84 us: shards(): lax.all_to_all(spread, 'row', split_axis=2, concat_axis=1, tiled=True)]
    dot_general x11 -> x0, matrix products: 15.2 us -> none  [the longest x3 9.01 us: mix(): jnp.dot(flat, packed(matrix, transposed), preferred_element_type=jnp.floa...]
    unnamed x17 -> x1, local copies, waits for them, and re-layouts: 12.4 us -> 2.26 us
    all_to_all x2 -> x0, starting transfers between devices: 9.57 us -> none  [the longest x1 5.12 us: shards(): lax.all_to_all(spread, 'row', split_axis=2, concat_axis=1, tiled=True)]
    reshape x4 -> x0, local copies, waits for them, and re-layouts: 6.23 us -> none  [the longest x2 4.72 us: mix(): mixed = mixed.astype(jnp.bfloat16).reshape(rows, groups, planes, width)]
    slice x4 -> x0, local copies, waits for them, and re-layouts: 5.52 us -> none  [contract(): real_part = dot(left[0], right[0]) - dot(left[1], right[1])]
    transpose x3 -> x0, local copies, waits for them, and re-layouts: 4.87 us -> none  [the longest x1 3.25 us: mix(): return mixed.transpose(2, 0, 1, 3).reshape(planes, rows, cols)]
  transfers between devices with their start and end apart: 2 -> 0, of which waited for: 2 -> 0; matrix products, arithmetic and copies ran while one was open for 6% -> 0% of each run, Pallas kernels for 0% -> 0%
where the time goes in v3:
time: 139 us
  Pallas kernels  134 us (96%)
  local copies, waits for them, and re-layouts  2.95 us (2%)
  other arithmetic  1.46 us (1%)
    pallas_call x1, Pallas kernels, fused(): pl.pallas_call(functools.partial(core_kernel, n, scale), out_shape=jax.Sh...  134 us

profile of v3, /device:TPU:13, one launch (start us, length us, event | category | flops | bytes accessed | tf_op | source)
XLA Modules:
  0.0 138.9 jit_solution(16692194314897149834)
XLA Ops:
  0.0 0.7 slice.7
  0.7 0.9 select_reduce_fusion
  1.6 0.6 pad_add_fusion.order_ref
  2.2 134.4 %shard_map.55 = f32[2,256,512]{2,1,0:T(8,128)} custom-call(bf16[2,256,4096]{2,1,0:T(8,128)(2,1)} %x_hbm.1, bf16[2,32,4096]{2,1,0:T(8,128)(2,1)} %right_ref.1, bf16[10,2,2,32,512]{4,3,2,1,0:T(8,128)(2,1)} %branch_ref.1, s32[10]{0:T(128)} %bits_ref.1, s32[5,8]{1,0:T(8,128)} %pad_add_fusion.order_ref), custom_call_target="tpu_custom_call" | custom-call | tf_op jit(solution)/shard_map/pallas_call | solution.py:370
  136.6 2.3 %copy.7 = f32[2,256,512]{2,1,0:T(8,128)} copy(f32[2,256,512]{2,1,0:T(8,128)} %shard_map.55) | data formatting | bytes 2097152
  (1 shorter events, 0.0 us)

commit v4 on v3

--- a/solution.py
+++ b/solution.py
@@ -77,54 +77,65 @@
         step = -distance if side == 0 else distance
         return ring_device(self.place + step, core, self.reach)
 
-    def copy(self, origin, half, slot, target):
-        ref = self.buf.at[origin] if half is None else self.buf.at[origin, half]
+    def copy(self, origin, plane, slot, target):
+        ref = self.buf.at[origin, plane]
         return pltpu.make_async_remote_copy(
             src_ref=ref, dst_ref=ref,
             send_sem=self.send_sems.at[slot], recv_sem=self.recv_sems.at[slot],
             device_id={"row": target}, device_id_type=pl.DeviceIdType.MESH,
         )
 
-    def ring_copy(self, side, distance):
-        half = side if distance == self.reach else None
+    def planes(self, side, distance):
+        return (side,) if distance == self.reach else (0, 1)
+
+    def slot(self, side, distance, plane):
+        return (side * self.reach + distance - 1) * 2 + plane
+
+    def ring_copy(self, side, distance, plane):
         origin = self.origin(side, distance - 1, self.core)
         target = self.right if side == 0 else self.left
-        return self.copy(origin, half, side * self.reach + distance - 1, target)
-
-    def ring_arrival(self, side, distance):
-        half = side if distance == self.reach else None
+        return self.copy(origin, plane, self.slot(side, distance, plane), target)
+
+    def ring_arrival(self, side, distance, plane):
         origin = self.origin(side, distance, self.core)
         target = self.right if side == 0 else self.left
-        return self.copy(origin, half, side * self.reach + distance - 1, target)
-
-    def twin_copy(self, side, distance, core):
-        half = side if distance == self.reach else None
+        return self.copy(origin, plane, self.slot(side, distance, plane), target)
+
+    def twin_copy(self, side, distance, plane, core):
         origin = self.origin(side, distance, core)
-        slot = 2 * self.reach if distance == 0 else 2 * self.reach + side * self.reach + distance
-        return self.copy(origin, half, slot, self.twin)
+        past = 4 * self.reach
+        slot = past + plane if distance == 0 else past + 2 + self.slot(side, distance, plane)
+        return self.copy(origin, plane, slot, self.twin)
 
     def start(self):
-        self.ring_copy(0, 1).start()
-        self.ring_copy(1, 1).start()
-        self.twin_copy(0, 0, self.core).start()
+        for plane in (0, 1):
+            self.ring_copy(0, 1, plane).start()
+            self.ring_copy(1, 1, plane).start()
+        for plane in (0, 1):
+            self.twin_copy(0, 0, plane, self.core).start()
 
     def step(self, distance):
-        for side in (0, 1):
-            self.ring_arrival(side, distance).wait_recv()
-            if distance < self.reach:
-                self.ring_copy(side, distance + 1).start()
-            self.twin_copy(side, distance, self.core).start()
+        for plane in (0, 1):
+            for side in (0, 1):
+                if plane in self.planes(side, distance):
+                    self.ring_arrival(side, distance, plane).wait_recv()
+                    if distance < self.reach and plane in self.planes(side, distance + 1):
+                        self.ring_copy(side, distance + 1, plane).start()
+                    self.twin_copy(side, distance, plane, self.core).start()
 
     def wait_twin(self, distance):
         for side in (0, 1) if distance else (0,):
-            self.twin_copy(side, distance, 1 - self.core).wait_recv()
+            for plane in self.planes(side, distance):
+                self.twin_copy(side, distance, plane, 1 - self.core).wait_recv()
 
     def finish(self):
         for distance in range(1, self.reach + 1):
             for side in (0, 1):
-                self.ring_copy(side, distance).wait_send()
-                self.twin_copy(side, distance, self.core).wait_send()
-        self.twin_copy(0, 0, self.core).wait_send()
+                for plane in self.planes(side, distance):
+                    self.ring_copy(side, distance, plane).wait_send()
+                    self.twin_copy(side, distance, plane, self.core).wait_send()
+        for plane in (0, 1):
+            self.twin_copy(0, 0, plane, self.core).wait_send()
 
 
 def cross(a_real, a_imag, w_real, w_imag, transposed):
@@ -235,8 +246,8 @@
         for g in range(groups):
             part = last[plane][g * rows : (g + 1) * rows]
             dbuf[me, plane, :, pl.ds(g * width, width)] = part.astype(jnp.bfloat16)
+    gd.start()
     gq.step(3)
-    gd.start()
     gq.step(reach)
     x_copy.wait()
 
@@ -366,7 +377,7 @@
     vmem = pl.BlockSpec(memory_space=pltpu.VMEM)
     smem = pl.BlockSpec(memory_space=pltpu.SMEM)
     bf16 = jnp.bfloat16
-    slots = 4 * (n // 4) + 1
+    slots = 8 * (n // 4) + 2
     return pl.pallas_call(
         functools.partial(core_kernel, n, scale),
         out_shape=jax.ShapeDtypeStruct((planes, tall, width), jnp.float32),

time: 139 us -> 140 us (level)
  no operation moved by 1% of the time
where the time goes in v4:
time: 140 us; the launch traced here: 139 us
  Pallas kernels  135 us (96%)
  local copies, waits for them, and re-layouts  2.95 us (2%)
  other arithmetic  1.46 us (1%)
    pallas_call x1, Pallas kernels, fused(): pl.pallas_call(functools.partial(core_kernel, n, scale), out_shape=jax.Sh...  135 us

profile of v4, /device:TPU:13, one launch (start us, length us, event | category | flops | bytes accessed | tf_op | source)
XLA Modules:
  0.0 139.3 jit_solution(12640041297365411513)
XLA Ops:
  0.0 0.7 slice.7
  0.7 0.9 select_reduce_fusion
  1.6 0.6 pad_add_fusion.order_ref
  2.2 134.8 %shard_map.55 = f32[2,256,512]{2,1,0:T(8,128)} custom-call(bf16[2,256,4096]{2,1,0:T(8,128)(2,1)} %x_hbm.1, bf16[2,32,4096]{2,1,0:T(8,128)(2,1)} %right_ref.1, bf16[10,2,2,32,512]{4,3,2,1,0:T(8,128)(2,1)} %branch_ref.1, s32[10]{0:T(128)} %bits_ref.1, s32[5,8]{1,0:T(8,128)} %pad_add_fusion.order_ref), custom_call_target="tpu_custom_call" | custom-call | tf_op jit(solution)/shard_map/pallas_call | solution.py:381
  137.0 2.3 %copy.7 = f32[2,256,512]{2,1,0:T(8,128)} copy(f32[2,256,512]{2,1,0:T(8,128)} %shard_map.55) | data formatting | bytes 2097152
  (1 shorter events, 0.0 us)

commit v5 on v4

--- a/solution.py
+++ b/solution.py
@@ -147,8 +147,8 @@
     return dot(a_real, w_real) - dot(a_imag, w_imag), dot(a_real, w_imag) + dot(a_imag, w_real)
 
 
-def core_kernel(n, scale, x_hbm, right_ref, branch_ref, bits_ref, order_ref, out_ref,
-                pbuf, qbuf, dbuf, xbuf, fbuf, sbuf, acc, near, far, wbuf, x_sem,
+def core_kernel(n, x_hbm, right_ref, branch_ref, bits_ref, order_ref, out_ref,
+                pbuf, qbuf, dbuf, ebuf, xbuf, fbuf, sbuf, acc, near, far, wbuf, x_sem,
                 send_sems, recv_sems, near_sems, far_sems):
     reach = n // 4
     me = lax.axis_index("row")
@@ -159,9 +159,10 @@
     x_copy.start()
     gathers = [
         Gather(buf, send_sems.at[i], recv_sems.at[i], reach)
-        for i, buf in enumerate((pbuf, qbuf, dbuf))
+        for i, buf in enumerate((pbuf, qbuf, dbuf, ebuf))
     ]
-    gp, gq, gd = gathers
+    gp, gq, gd, ge = gathers
+    early = qbuf.shape[2]
 
     barrier = pltpu.get_barrier_semaphore()
 
@@ -174,7 +175,11 @@
     for s in range(sweeps):
         for plane in (0, 1):
             pbuf[me, plane, s] = branch_ref[2 * s, bits_ref[2 * s], plane]
-            qbuf[me, plane, s] = branch_ref[2 * s + 1, bits_ref[2 * s + 1], plane]
+            row_part = branch_ref[2 * s + 1, bits_ref[2 * s + 1], plane]
+            if s < early:
+                qbuf[me, plane, s] = row_part
+            else:
+                ebuf[me, plane, s - early] = row_part
     pl.semaphore_wait(barrier, n - 1)
     gp.start()
 
@@ -212,6 +217,12 @@
     def branch(s):
         return [pbuf[:, plane, s].reshape(width, width) for plane in (0, 1)]
 
+    def undo(s, group):
+        place = jnp.int32(0)
+        for g in range(1, groups):
+            place = jnp.where(order_ref[s, g] == group, jnp.int32(g), place)
+        return place
+
     def keep(pair, ref):
         for plane in (0, 1):
             ref[plane] = pair[plane].reshape(groups, rows, width).astype(ref.dtype)
@@ -235,13 +246,13 @@
     keep(cross(*operand(lambda g: order_ref[3, g]), *w4, False), sbuf)
     gq.step(1)
     w2 = [turned_rows(w) for w in branch(2)]
-    keep(cross(*operand(lambda g: order_ref[4, order_ref[2, g]]), *w2, True), fbuf)
-    exchange(lambda i: order_ref[1, i])
+    keep(cross(*operand(lambda g: order_ref[4, undo(2, g)]), *w2, True), fbuf)
+    exchange(lambda i: undo(1, i))
     gq.step(2)
     keep(cross(*operand(lambda g: g), *branch(1), True), fbuf)
     exchange(lambda i: i)
     w0 = [turned_cols(w) for w in branch(0)]
-    last = cross(*operand(lambda g: order_ref[0, g]), *w0, True)
+    last = cross(*operand(lambda g: undo(0, g)), *w0, True)
     for plane in (0, 1):
         for g in range(groups):
             part = last[plane][g * rows : (g + 1) * rows]
@@ -302,24 +313,26 @@
     join([me, gd.twin], own=True)
     for d in range(1, reach):
         gd.step(d)
+        if d == reach - 1:
+            ge.start()
         gd.wait_twin(d)
         join([gd.origin(side, d, core) for side in (0, 1) for core in (0, 1)])
     for d in range(reach + 1):
         gq.wait_twin(d)
 
     def row_factor(s):
-        return [qbuf[:, plane, s].reshape(width, width) for plane in (0, 1)]
+        buf, at = (qbuf, s) if s < early else (ebuf, s - early)
+        return [buf[:, plane, at].reshape(width, width) for plane in (0, 1)]
 
     q1 = [turned_rows(w) for w in row_factor(0)]
     q5 = [turned_cols(w) for w in row_factor(2)]
-    ends = cross(*row_factor(4), *row_factor(3), False)
     for plane in (0, 1):
         wbuf[0, plane] = q1[plane]
         wbuf[1, plane] = q5[plane]
-        wbuf[2, plane] = ends[plane].astype(wbuf.dtype)
     gd.step(reach)
     gd.wait_twin(reach)
     join([gd.origin(0, reach, core) for core in (0, 1)])
+    ge.step(1)
     arrivals(turn_one)
 
     pieces = n // groups
@@ -335,8 +348,10 @@
     ]
     keep(cross(*whole, wbuf[0, 0], wbuf[0, 1], True), fbuf)
     exchange(lambda i: i)
+    ge.step(2)
     keep(cross(*operand(lambda g: g), *row_factor(1), True), fbuf)
     exchange(lambda i: i)
+    ge.step(3)
     mixed = cross(*operand(lambda g: g), wbuf[1, 0], wbuf[1, 1], True)
     tall = width // pieces
     for plane in (0, 1):
@@ -350,6 +365,12 @@
         target = lax.rem(me + i, n)
         trade(turn_two, target, target).start()
 
+    ge.step(reach)
+    for d in range(reach + 1):
+        ge.wait_twin(d)
+    ends = cross(*row_factor(4), *row_factor(3), False)
+    for plane in (0, 1):
+        wbuf[2, plane] = ends[plane].astype(wbuf.dtype)
     arrivals(turn_two)
 
     amplitude = cross(
@@ -357,7 +378,7 @@
         wbuf[2, 0], wbuf[2, 1], True,
     )
     for plane in (0, 1):
-        out_ref[plane] = amplitude[plane] * scale
+        out_ref[plane] = amplitude[plane]
 
     for turn_at in (turn_one, turn_two):
 
@@ -369,7 +390,7 @@
         gather.finish()
 
 
-def fused(n, scale, left_stem, right_stem, branches, bits, order):
+def fused(n, left_stem, right_stem, branches, bits, order):
     planes, tall, cols = left_stem.shape
     rows = right_stem.shape[1]
     part, width = branches.shape[3:]
@@ -379,14 +400,15 @@
     bf16 = jnp.bfloat16
     slots = 8 * (n // 4) + 2
     return pl.pallas_call(
-        functools.partial(core_kernel, n, scale),
+        functools.partial(core_kernel, n),
         out_shape=jax.ShapeDtypeStruct((planes, tall, width), jnp.float32),
         in_specs=[pl.BlockSpec(memory_space=pl.ANY), vmem, vmem, smem, smem],
         out_specs=vmem,
         scratch_shapes=[
             pltpu.VMEM((n, planes, sweeps, part, width), bf16),
-            pltpu.VMEM((n, planes, sweeps, part, width), bf16),
+            pltpu.VMEM((n, planes, 3, part, width), bf16),
             pltpu.VMEM((n, planes, rows, cols), bf16),
+            pltpu.VMEM((n, planes, sweeps - 3, part, width), bf16),
             pltpu.VMEM((planes, tall, cols), bf16),
             pltpu.VMEM((planes, groups, rows, width), jnp.float32),
             pltpu.VMEM((planes, groups, rows, width), bf16),
@@ -395,8 +417,8 @@
             pltpu.VMEM((2, n, planes, rows, tall), bf16),
             pltpu.VMEM((3, planes, width, width), bf16),
             pltpu.SemaphoreType.DMA,
-            pltpu.SemaphoreType.DMA((3, slots)),
-            pltpu.SemaphoreType.DMA((3, slots)),
+            pltpu.SemaphoreType.DMA((4, slots)),
+            pltpu.SemaphoreType.DMA((4, slots)),
             pltpu.SemaphoreType.DMA((2, n)),
             pltpu.SemaphoreType.DMA((2, n)),
         ],
@@ -422,11 +444,7 @@
 
     scale = (2.0 * left_stem.shape[2]) ** (-0.5)
     if fits(n, left_stem, right_stem, branches, perms):
-        numbers = jnp.arange(perms.shape[1], dtype=jnp.int32)
-        hit = (perms[:, None, :] == numbers[None, :, None]).astype(jnp.int32)
-        undo = jnp.sum(hit * numbers, axis=2)
-        order = jnp.concatenate([undo[:left_sweeps], perms[left_sweeps:]])
-        return fused(n, scale, left_stem, right_stem, branches, slice_bits, order)
+        return fused(n, left_stem, right_stem, branches, slice_bits, perms) * scale
 
     def own(index):
         return lax.dynamic_index_in_dim(branches[index], slice_bits[index], 0, keepdims=False)

time: 140 us -> 136 us (0.971)
  local copies, waits for them, and re-layouts: 2.95 us -> 0 us
    mul x0 -> x1, other arithmetic: none -> 2.31 us  [shards(): return fused(n, left_stem, right_stem, branches, slice_bits, perms) * scale]
    unnamed x1 -> x0, local copies, waits for them, and re-layouts: 2.26 us -> none
where the time goes in v5:
time: 136 us
  Pallas kernels  134 us (99%)
  other arithmetic  2.31 us (2%)
    pallas_call x1, Pallas kernels, fused(): pl.pallas_call(functools.partial(core_kernel, n), out_shape=jax.ShapeDtyp...  134 us

profile of v5, /device:TPU:13, one launch (start us, length us, event | category | flops | bytes accessed | tf_op | source)
XLA Modules:
  0.0 136.0 jit_solution(7783561450960646887)
XLA Ops:
  0.0 133.7 %shard_map.55 = f32[2,256,512]{2,1,0:T(8,128)} custom-call(bf16[2,256,4096]{2,1,0:T(8,128)(2,1)} %x_hbm.1, bf16[2,32,4096]{2,1,0:T(8,128)(2,1)} %right_ref.1, bf16[10,2,2,32,512]{4,3,2,1,0:T(8,128)(2,1)} %branch_ref.1, s32[10]{0:T(128)} %bits_ref.1, s32[5,8]{1,0:T(8,128)} %order_ref.1), custom_call_target="tpu_custom_call" | custom-call | tf_op jit(solution)/shard_map/pallas_call | solution.py:402
  133.7 2.3 %broadcast_multiply_fusion = f32[2,256,512]{2,1,0:T(8,128)} fusion(f32[2,256,512]{2,1,0:T(8,128)} %shard_map.55), kind=kLoop, calls=%fused_computation | loop fusion | flops 262144 | bytes 2097152 | tf_op jit(solution)/shard_map/mul | solution.py:447

commit v6 on v5

--- a/solution.py
+++ b/solution.py
@@ -406,9 +406,9 @@
         out_specs=vmem,
         scratch_shapes=[
             pltpu.VMEM((n, planes, sweeps, part, width), bf16),
-            pltpu.VMEM((n, planes, 3, part, width), bf16),
+            pltpu.VMEM((n, planes, sweeps - 1, part, width), bf16),
             pltpu.VMEM((n, planes, rows, cols), bf16),
-            pltpu.VMEM((n, planes, sweeps - 3, part, width), bf16),
+            pltpu.VMEM((n, planes, 1, part, width), bf16),
             pltpu.VMEM((planes, tall, cols), bf16),
             pltpu.VMEM((planes, groups, rows, width), jnp.float32),
             pltpu.VMEM((planes, groups, rows, width), bf16),

time: 136 us -> 137 us (level)
  no operation moved by 1% of the time
where the time goes in v6:
time: 137 us
  Pallas kernels  135 us (99%)
  other arithmetic  2.31 us (2%)
    pallas_call x1, Pallas kernels, fused(): pl.pallas_call(functools.partial(core_kernel, n), out_shape=jax.ShapeDtyp...  135 us

profile of v6, /device:TPU:13, one launch (start us, length us, event | category | flops | bytes accessed | tf_op | source)
XLA Modules:
  0.0 137.1 jit_solution(3429707714661840569)
XLA Ops:
  0.0 134.8 %shard_map.55 = f32[2,256,512]{2,1,0:T(8,128)} custom-call(bf16[2,256,4096]{2,1,0:T(8,128)(2,1)} %x_hbm.1, bf16[2,32,4096]{2,1,0:T(8,128)(2,1)} %right_ref.1, bf16[10,2,2,32,512]{4,3,2,1,0:T(8,128)(2,1)} %branch_ref.1, s32[10]{0:T(128)} %bits_ref.1, s32[5,8]{1,0:T(8,128)} %order_ref.1), custom_call_target="tpu_custom_call" | custom-call | tf_op jit(solution)/shard_map/pallas_call | solution.py:402
  134.8 2.3 %broadcast_multiply_fusion = f32[2,256,512]{2,1,0:T(8,128)} fusion(f32[2,256,512]{2,1,0:T(8,128)} %shard_map.55), kind=kLoop, calls=%fused_computation | loop fusion | flops 262144 | bytes 2097152 | tf_op jit(solution)/shard_map/mul | solution.py:447
